TPU v7x, 256 devices: a whole 4x4x8 slice. The times are simulated.
256 devices in a mesh: dp: 16 (over x_lo, y, core), mp: 16 (over x_hi, z).
Axes of the slice: x: 4 (x_hi: 2, x_lo: 2; x = x_hi * 2 + x_lo), y: 4, z: 8, core: 2. Of those that a mesh axis runs over, the one named last changes fastest.
Arguments:
- patches: bfloat16 [8192, 6144], P('dp', 'mp'), may hold values from -1000 to 1000
- norm_gain: bfloat16 [6144], P('mp'), may hold values from 0.099609375 to 1.8984375
- qkv_weight: bfloat16 [6144, 12288], P(None, 'mp'), may hold values from -0.078125 to 0.078125
- qk_gain: float32 [2, 32, 128], P(None, 'mp'), may hold values from 0.6 to 5.5
- context_grad: bfloat16 [8192, 4096], P('dp', 'mp'), may hold values from -6 to 6
Outputs:
- context: bfloat16 [8192, 4096], P('dp', 'mp')
- input_grad: bfloat16 [8192, 6144], P('dp', 'mp')
- weight_grad: bfloat16 [6144, 12288], P('dp', 'mp')
- norm_gain_grad: float32 [6144], P('mp')
- qk_gain_grad: float32 [2, 32, 128], P(None, 'mp')
All inputs are finite; a program needn't handle non-finite values.
Results may differ from a plain program's by a relative error of at most 0.025.
The roundings to bfloat16 on the way count: a program that leaves them out, or rounds other values in their place, can miss the bound.
Values may be sent and summed in bfloat16 or wider, within the bound.
A program may use at most 128 MiB of HBM per device.

v0:
```python
import math

import jax
import jax.numpy as jnp
from jax import lax
from jax.sharding import PartitionSpec as P

HEAD_DIM = 128
PATCHES = 256


epsilon = 1e-06


def head_norm(values):
    centered = values - jnp.mean(values, axis=-1, keepdims=True)
    inv_std = lax.rsqrt(jnp.mean(centered * centered, axis=-1, keepdims=True) + epsilon)
    return (centered * inv_std, inv_std)


def norm_back(incoming_grad, unit_vals, inv_std):
    mean_grad = jnp.mean(incoming_grad, axis=-1, keepdims=True)
    second = jnp.mean(incoming_grad * unit_vals, axis=-1, keepdims=True)
    return inv_std * (incoming_grad - mean_grad - unit_vals * second)


def attend(packed, head_gains, incoming_grad):
    q_unit, q_inv = head_norm(packed[:, :, 0])
    k_unit, k_inv = head_norm(packed[:, :, 1])
    query_normed = (q_unit * head_gains[0]).astype(jnp.bfloat16)
    key_normed = (k_unit * head_gains[1]).astype(jnp.bfloat16)
    value_narrow = packed[:, :, 2].astype(jnp.bfloat16)
    scale_factor = 1.0 / math.sqrt(packed.shape[-1])
    logit_scores = (
        jnp.einsum("tih,tjh->tij", query_normed, key_normed, preferred_element_type=jnp.float32)
        * scale_factor
    )
    shifted = logit_scores - jnp.max(logit_scores, axis=-1, keepdims=True)
    exp_scores = jnp.exp(shifted)
    attn_probs = exp_scores / jnp.sum(exp_scores, axis=-1, keepdims=True)
    probability_narrow = attn_probs.astype(jnp.bfloat16)
    context = jnp.einsum(
        "rin,rnt->rit", probability_narrow, value_narrow, preferred_element_type=jnp.float32
    ).astype(jnp.bfloat16)
    probability_grad = jnp.einsum(
        "tih,tjh->tij", incoming_grad, value_narrow, preferred_element_type=jnp.float32
    )
    value_grad = jnp.einsum(
        "smi,smy->siy", probability_narrow, incoming_grad, preferred_element_type=jnp.float32
    )
    row_delta = jnp.sum(attn_probs * probability_grad, axis=-1, keepdims=True)
    score_grad = (attn_probs * (probability_grad - row_delta)).astype(jnp.bfloat16)
    normed_query_grad = (
        jnp.einsum("rin,rnt->rit", score_grad, key_normed, preferred_element_type=jnp.float32)
        * scale_factor
    )
    normed_key_grad = (
        jnp.einsum("smi,smy->siy", score_grad, query_normed, preferred_element_type=jnp.float32)
        * scale_factor
    )
    gain_grad = jnp.stack(
        [
            jnp.sum(normed_query_grad * q_unit, axis=(0, 1)),
            jnp.sum(normed_key_grad * k_unit, axis=(0, 1)),
        ]
    )
    d_query = norm_back(normed_query_grad * head_gains[0], q_unit, q_inv)
    d_key = norm_back(normed_key_grad * head_gains[1], k_unit, k_inv)
    packed_grad = jnp.stack([d_query, d_key, value_grad], axis=2).astype(jnp.bfloat16)
    return (context, packed_grad, gain_grad)


def per_device(patches, norm_gain, qkv_weight, qk_gain, context_grad):
    tok_rows, shard_width = patches.shape
    full_width = shard_width * lax.axis_size("mp")
    head_cols = qkv_weight.shape[1]
    row_vals = patches.astype(jnp.float32)
    gain_wide = norm_gain.astype(jnp.float32)
    row_mean = lax.psum(jnp.sum(row_vals, axis=1), "mp")[:, None] / full_width
    centered = row_vals - row_mean
    row_var = lax.psum(jnp.sum(centered * centered, axis=1), "mp")[:, None] / full_width
    inv_std = lax.rsqrt(row_var + epsilon)
    unit_rows = centered * inv_std
    normed = (unit_rows * gain_wide).astype(jnp.bfloat16)
    piece = lax.all_gather(normed, "mp", axis=1, tiled=True)
    acc_proj = jnp.dot(piece, qkv_weight, preferred_element_type=jnp.float32)
    img_count = tok_rows // PATCHES
    heads_here = head_cols // (3 * HEAD_DIM)
    packed = acc_proj.reshape(img_count, PATCHES, heads_here, 3, HEAD_DIM).transpose(2, 0, 1, 3, 4)
    incoming_grad = context_grad.reshape(img_count, PATCHES, heads_here, HEAD_DIM).transpose(
        2, 0, 1, 3
    )
    head_gains = qk_gain.transpose(1, 0, 2)
    context, packed_grad, gain_grad = jax.vmap(attend)(packed, head_gains, incoming_grad)
    context_out = context.transpose(1, 2, 0, 3).reshape(tok_rows, heads_here * HEAD_DIM)
    qkv_grad = packed_grad.transpose(1, 2, 0, 3, 4).reshape(tok_rows, head_cols)
    feature_terms = lax.dot_general(
        qkv_grad, qkv_weight, (((1,), (1,)), ((), ())), preferred_element_type=jnp.float32
    )
    normed_grad = lax.psum_scatter(
        feature_terms.astype(jnp.bfloat16), "mp", scatter_dimension=1, tiled=True
    ).astype(jnp.float32)
    back_grad = normed_grad * gain_wide
    mean_grad, cross_grad = lax.psum(
        (jnp.sum(back_grad, axis=1), jnp.sum(back_grad * unit_rows, axis=1)), "mp"
    )
    input_grad = (
        inv_std
        * (
            back_grad
            - mean_grad[:, None] / full_width
            - unit_rows * cross_grad[:, None] / full_width
        )
    ).astype(jnp.bfloat16)
    norm_gain_grad, qk_gain_grad = lax.psum(
        (jnp.sum(normed_grad * unit_rows, axis=0), gain_grad.transpose(1, 0, 2)), "dp"
    )
    weight_grad = lax.psum_scatter(
        lax.dot_general(
            piece, qkv_grad, (((0,), (0,)), ((), ())), preferred_element_type=jnp.float32
        ),
        "dp",
        scatter_dimension=0,
        tiled=True,
    )
    return (context_out, input_grad, weight_grad.astype(jnp.bfloat16), norm_gain_grad, qk_gain_grad)


def solution(mesh):
    in_specs = (P("dp", "mp"), P("mp"), P(None, "mp"), P(None, "mp", None), P("dp", "mp"))
    out_specs = (P("dp", "mp"), P("dp", "mp"), P("dp", "mp"), P("mp"), P(None, "mp", None))
    return jax.shard_map(
        per_device, mesh=mesh, in_specs=in_specs, out_specs=out_specs, check_vma=False
    )
```

profile of v0, /device:TPU:1, one launch (start us, length us, event | category | flops | bytes accessed | tf_op | source)
XLA Modules:
  0.0 592.6 jit_solution(3250310204606394387)
XLA Ops:
  7.9 1.1 convert_reduce_fusion
  9.0 38.5 %psum.42 = f32[512]{0:T(512)S(1)} all-reduce(f32[512]{0:T(512)S(1)} %convert_reduce_fusion), channel_id=1, replica_groups=mesh['dp'=16,'mp'=16] {'mp'}, use_global_device_ids=true, to_apply=%region_1.0 | all-reduce | flops 512 | bytes 4096 | tf_op jit(solution)/shard_map/psum | solution.py:79
  47.6 1.2 fusion.17
  48.8 29.7 %psum.43 = f32[512]{0:T(512)S(1)} all-reduce(f32[512]{0:T(512)S(1)} %fusion.17), channel_id=1, replica_groups=mesh['dp'=16,'mp'=16] {'mp'}, use_global_device_ids=true, to_apply=%region_3.0 | all-reduce | flops 512 | bytes 4096 | tf_op jit(solution)/shard_map/psum | solution.py:81
  78.5 2.0 fusion.12
  80.5 1.0 reshape.80
  83.0 130.7 %all-gather.2.cloned.1.call-done = bf16[512,6144]{1,0:T(8,128)(2,1)} async-done(((bf16[512,384]{1,0:T(8,128)(2,1)}), bf16[512,6144]{1,0:T(8,128)(2,1)}) %all-gather.2.cloned.1.call-update) | async-done | bytes 6291472 | tf_op jit(solution)/shard_map/all_gather | solution.py:85
  213.7 9.5 %fusion.36 = f32[512,768]{0,1:T(8,128)S(1)} fusion(bf16[512,6144]{1,0:T(8,128)(2,1)} %all-gather.2.cloned.1.call-done, bf16[6144,768]{1,0:T(8,128)(2,1)} %param.7), kind=kOutput, calls=%fused_computation.81 | convolution fusion | flops 4831838208 | bytes 17301504 | tf_op jit(solution)/shard_map/dot_general | solution.py:86
  223.2 1.0 reshape.78
  224.2 0.7 copy.36
  227.3 1.4 fusion.4
  229.5 1.8 multiply_reduce_fusion.2
  231.4 1.3 fusion.22
  233.6 10.8 %convolution_convert_fusion = bf16[512,6144]{1,0:T(8,128)(2,1)} fusion(bf16[512,768]{0,1:T(8,128)(2,1)S(1)} %bitcast.105, bf16[6144,768]{1,0:T(8,128)(2,1)} %param.7), kind=kOutput, calls=%fused_computation.1 | convolution fusion | flops 4834983936 | bytes 16515072 | tf_op jit(solution)/shard_map/dot_general | solution.py:97
  244.4 8.6 %copy.57 = bf16[512,6144]{0,1:T(8,128)(2,1)} copy(bf16[512,6144]{1,0:T(8,128)(2,1)} %convolution_convert_fusion) | data formatting | bytes 12582912
  253.2 11.9 %fusion.38 = f32[6144,768]{1,0:T(8,128)} fusion(bf16[512,6144]{1,0:T(8,128)(2,1)} %all-gather.2.cloned.1.call-done, bf16[512,768]{0,1:T(8,128)(2,1)S(1)} %bitcast.106), kind=kOutput, calls=%fused_computation.83 | convolution fusion | flops 4831838208 | bytes 25952256 | tf_op jit(solution)/shard_map/dot_general | solution.py:119
  265.2 1.8 fusion.3
  268.0 201.0 %reduce-scatter.7.cloned.1.call-done = bf16[384,512]{1,0:T(8,128)(2,1)} async-done(((bf16[6144,512]{1,0:T(8,128)(2,1)}), bf16[384,512]{1,0:T(8,128)(2,1)}) %reduce-scatter.7.cloned.1.call-update) | async-done | bytes 393232
  469.0 1.2 copy.58
  470.8 31.6 %all-reduce.1 = (f32[384]{0:T(512)}, f32[2,2,128]{2,1,0:T(2,128)}) all-reduce(f32[384]{0:T(512)S(1)} %get-tuple-element.15, f32[2,2,128]{2,1,0:T(2,128)S(1)} %pad_maximum_fusion), channel_id=1, replica_groups=mesh['dp'=16,'mp'=16] {'dp'}, use_global_device_ids=true, to_apply=%region_22.0 | all-reduce | flops 896 | bytes 7168 | tf_op jit(solution)/shard_map/psum | solution.py:115
  502.5 32.5 %all-reduce = (f32[512]{0:T(512)S(1)}, f32[512]{0:T(512)S(1)}) all-reduce(f32[512]{0:T(512)S(1)} %get-tuple-element.16, f32[512]{0:T(512)S(1)} %get-tuple-element.19), channel_id=1, replica_groups=mesh['dp'=16,'mp'=16] {'mp'}, use_global_device_ids=true, to_apply=%region_19.0 | all-reduce | flops 1024 | bytes 8192 | tf_op jit(solution)/shard_map/psum | solution.py:104
  535.0 1.1 fusion.16
  536.1 47.8 %reduce-scatter.5.cloned.1.call-done = f32[384,768]{1,0:T(8,128)} async-done(((f32[6144,768]{1,0:T(8,128)}), f32[384,768]{1,0:T(8,128)}) %reduce-scatter.5.cloned.1.call-update) | async-done | bytes 1179664 | tf_op jit(solution)/shard_map/reduce_scatter | solution.py:118
  583.9 2.1 convert_element_type.58
  (39 shorter events, 8.1 us)
Async XLA Ops:
  7.2 206.5 %all-gather.2.cloned.1.call-start = ((), (), s32[]{:S(2)}) async-start(), calls=%async_computation.2 | async-start | bytes 6684672 | tf_op jit(solution)/shard_map/all_gather | solution.py:85
  80.5 388.5 %reduce-scatter.7.cloned.1.call-start = ((), (), s32[]{:S(2)}) async-start(), calls=%async_computation.4 | async-start | bytes 6684672
  226.8 2.8 copy-start.1
  228.7 3.9 copy-start.2
  253.0 330.9 %reduce-scatter.5.cloned.1.call-start = ((), (), s32[]{:S(2)}) async-start(), calls=%async_computation.3 | async-start | bytes 20054016 | tf_op jit(solution)/shard_map/reduce_scatter | solution.py:118
  265.2 205.0 %copy-start = (bf16[512,384]{1,0:T(8,128)(2,1)S(1)}, bf16[512,384]{1,0:T(8,128)(2,1)}, u32[]{:S(2)}) copy-start(bf16[512,384]{1,0:T(8,128)(2,1)} %param.5) | copy-start | bytes 1179652
Sparse Core Ops, SparseCore 0:
  80.6 132.9 all-gather.1
  253.1 215.8 reduce-scatter.6
  471.8 112.1 reduce-scatter.4
where the time goes:
time: 594 us; the launch traced here: 593 us
  waiting for transfers between devices  380 us (64%)
  blocking collectives  132 us (22%)
  matrix products  38.4 us (6%)
  local copies, waits for them, and re-layouts  15.1 us (3%)
  between operations  14 us (2%)
  other arithmetic  12.9 us (2%)
    unnamed x4, waiting for transfers between devices  201 us
    all_gather x1, waiting for transfers between devices, per_device(): piece = lax.all_gather(normed, 'mp', axis=1, tiled=True)  131 us
    reduce_scatter x1, waiting for transfers between devices, per_device(): lax.psum_scatter(lax.dot_general(piece, qkv_grad, (((0,), (0,)), ((), ())...  47.8 us
    psum x1, blocking collectives, per_device(): row_mean = lax.psum(jnp.sum(row_vals, axis=1), 'mp')[:, None] / full_width  38.5 us
    psum x1, blocking collectives, per_device(): lax.psum((jnp.sum(back_grad, axis=1), jnp.sum(back_grad * unit_rows, axis...  32.5 us
    psum x1, blocking collectives, per_device(): lax.psum((jnp.sum(normed_grad * unit_rows, axis=0), gain_grad.transpose(1...  31.6 us
    psum x1, blocking collectives, per_device(): lax.psum(jnp.sum(centered * centered, axis=1), 'mp')[:, None] / full_width  29.7 us
    dot_general x1, matrix products, per_device(): lax.dot_general(piece, qkv_grad, (((0,), (0,)), ((), ())), preferred_elem...  11.9 us
  transfers between devices with their start and end apart: 3, of which 3 were waited for; matrix products, arithmetic and copies ran while one was open for 3% of the time, Pallas kernels for 0%

commit v1 on v0

v1 whole, which is shorter than its diff:
```python
import functools
import math

import jax
import jax.numpy as jnp
from jax import lax
from jax.experimental import pallas as pl
from jax.experimental.pallas import tpu as pltpu
from jax.sharding import PartitionSpec as P

HEAD_DIM = 128
IMG = 256
NIMG = 2
TOK = IMG * NIMG
FB = 384
NB = 16
D = FB * NB
HC = 768
GR = 16
ROWS = GR + TOK
HALF = IMG // 2
XC = 384
EPS = 1e-6
SCALE = 1.0 / math.sqrt(HEAD_DIM)
MESH = pl.DeviceIdType.MESH
F32 = jnp.float32
BF16 = jnp.bfloat16
NSEM = 192


def dot_t(a, b):
    return lax.dot_general(a, b, (((1,), (1,)), ((), ())), preferred_element_type=F32)


def t_dot(a, b):
    return lax.dot_general(a, b, (((0,), (0,)), ((), ())), preferred_element_type=F32)


def kernel(
    p_hbm, gain_ref, w_hbm, qkg_ref, cg_ref,
    ctx_ref, ig_ref, wg_ref, small_ref,
    xg, wv, nrm, nrm_t, proj, qkvg, mu, inv,
    cr, ci, t1, cxs, cxr, cys, cyr, plane1,
    ds, dr, dxr, dxl, dyr,
    sxs, sxr, trans, sms, smr,
    ss, rs, ls,
):
    d = lax.axis_index("dp")
    m = lax.axis_index("mp")
    xl, y, core = d // 8, (d // 2) % 4, d % 2
    xh, z = m // 8, m % 8
    count = [0]
    sends = []

    def at(xl_=None, y_=None, core_=None, xh_=None, z_=None):
        xl_ = xl if xl_ is None else xl_
        y_ = y if y_ is None else y_
        core_ = core if core_ is None else core_
        xh_ = xh if xh_ is None else xh_
        z_ = z if z_ is None else z_
        return {"dp": xl_ * 8 + y_ * 2 + core_, "mp": xh_ * 8 + z_}

    z_dev = {1: at(z_=(z + 1) % 8), -1: at(z_=(z + 7) % 8)}
    y_dev = {1: at(y_=(y + 1) % 4), -1: at(y_=(y + 3) % 4)}
    xh_dev = at(xh_=1 - xh)
    xl_dev = at(xl_=1 - xl)
    core_dev = at(core_=1 - core)

    def send(src, dst, dev):
        i = count[0]
        count[0] += 1
        copy = pltpu.make_async_remote_copy(
            src_ref=src, dst_ref=dst, send_sem=ss.at[i], recv_sem=rs.at[i],
            device_id=dev, device_id_type=MESH,
        )
        copy.start()
        sends.append(copy)
        return copy

    own = pltpu.make_async_copy(p_hbm, xg.at[m, pl.ds(GR, TOK)], ls.at[0])
    own.start()
    weights = pltpu.make_async_copy(w_hbm, wv, ls.at[1])
    weights.start()
    xg[m, pl.ds(0, GR), :] = jnp.broadcast_to(gain_ref[...], (GR, FB))
    barrier = pltpu.get_barrier_semaphore()
    for o in range(1, NB):
        pl.semaphore_signal(barrier, inc=1, device_id={"dp": d, "mp": (m + o) % NB}, device_id_type=MESH)
        pl.semaphore_signal(barrier, inc=1, device_id={"dp": (d + o) % NB, "mp": m}, device_id_type=MESH)
    pl.semaphore_wait(barrier, 2 * (NB - 1))
    own.wait()

    def blk(plane, zz):
        return (xh if plane == 0 else 1 - xh) * 8 + (zz + 16) % 8

    def span(img, part):
        lo0 = 0 if img == 0 else GR + IMG
        mid = GR + img * IMG + HALF
        end = GR + (img + 1) * IMG
        return {
            "full": (lo0, end - lo0),
            "lo": (lo0, mid - lo0),
            "hi": (mid, end - mid),
            "hi0": (mid, HALF // 2),
            "hi1": (mid + HALF // 2, HALF // 2),
        }[part]

    ring = {}
    xrecv = {0: [], 1: []}

    def send_block(img, plane, origin_z, part, dev):
        r, n = span(img, part)
        ref = xg.at[blk(plane, origin_z), pl.ds(r, n)]
        return send(ref, ref, dev)

    def hop_parts(plane):
        if plane == 0:
            return {1: "full", -1: "full"}, {1: "lo", -1: "hi"}
        return {1: "hi", -1: "hi"}, {1: "hi0", -1: "hi1"}

    def forward(img, plane, s):
        parts = hop_parts(plane)[0 if s < 4 else 1]
        for dr_ in (1, -1):
            ring[(img, plane, s, dr_)] = send_block(img, plane, z - (s - 1) * dr_, parts[dr_], z_dev[dr_])

    def arrive(img, plane, s):
        for dr_ in (1, -1):
            ring[(img, plane, s, dr_)].wait_recv()

    def ag0(img):
        ring[(img, "x")] = send_block(img, 0, z, "hi", xh_dev)
        forward(img, 0, 1)
        xrecv[img].append(send_block(img, 0, z, "lo", xh_dev))

    def ag1(img):
        ring[(img, "x")].wait_recv()
        forward(img, 1, 1)

    def ag_hop(img, plane, s):
        arrive(img, plane, s)
        if s < 4:
            forward(img, plane, s + 1)
        if plane == 0:
            for dr_ in (1, -1) if s < 4 else (1,):
                xrecv[img].append(send_block(img, 0, z - s * dr_, "lo", xh_dev))

    def ag_end(img):
        for c in xrecv[img]:
            c.wait_recv()

    def norm(img):
        @pl.loop(0, IMG // 64)
        def _(c):
            r = pl.ds(pl.multiple_of(GR + img * IMG + c * 64, 16), 64)
            shift = jnp.mean(xg[0, r, :].astype(F32), axis=1, keepdims=True)

            def stat(k, carry):
                v = xg[k, r, :].astype(F32) - shift
                w = v * v
                fold = lambda t: t[:, :128] + t[:, 128:256] + t[:, 256:]
                return carry[0] + fold(v), carry[1] + fold(w)

            zero = jnp.zeros((64, 128), F32)
            s1, s2 = lax.fori_loop(0, NB, stat, (zero, zero))
            off = jnp.sum(s1, axis=1, keepdims=True) / D
            var = jnp.sum(s2, axis=1, keepdims=True) / D - off * off
            mean = shift + off
            rstd = lax.rsqrt(jnp.maximum(var, 0.0) + EPS)
            mu[r, :] = mean
            inv[r, :] = rstd

            def put(k, _):
                g = xg[k, pl.ds(0, 1), :].astype(F32)
                unit = (xg[k, r, :].astype(F32) - mean) * rstd
                nrm[r, pl.ds(pl.multiple_of(k * FB, 128), FB)] = (unit * g).astype(BF16)
                return 0

            lax.fori_loop(0, NB, put, 0)

        if img == 0:
            @pl.loop(0, NB)
            def _(k):
                nrm[pl.ds(0, GR), pl.ds(pl.multiple_of(k * FB, 128), FB)] = xg[k, pl.ds(0, GR), :]

    def project(img):
        r = slice(0, GR + IMG) if img == 0 else slice(GR + IMG, ROWS)

        @pl.loop(0, HC // 256)
        def _(c):
            cols = pl.ds(pl.multiple_of(c * 256, 256), 256)
            proj[r, cols] = jnp.dot(nrm[r, :], wv[:, cols], preferred_element_type=F32)

    def transpose(img):
        @pl.loop(0, NB)
        def _(k):
            cols = pl.ds(pl.multiple_of(k * FB, 128), FB)
            rows = slice(GR + img * IMG, GR + (img + 1) * IMG)
            nrm_t[cols, img * IMG:(img + 1) * IMG] = nrm[rows, cols].T

    def head_norm(v):
        cen = v - jnp.mean(v, axis=1, keepdims=True)
        rstd = lax.rsqrt(jnp.mean(cen * cen, axis=1, keepdims=True) + EPS)
        return cen * rstd, rstd

    def norm_back(g, unit, rstd):
        return rstd * (
            g - jnp.mean(g, axis=1, keepdims=True) - unit * jnp.mean(g * unit, axis=1, keepdims=True)
        )

    def attend(img, h):
        r = slice(GR + img * IMG, GR + (img + 1) * IMG)
        rows = slice(img * IMG, (img + 1) * IMG)
        c0 = h * 3 * HEAD_DIM
        cols = [slice(c0 + i * HEAD_DIM, c0 + (i + 1) * HEAD_DIM) for i in range(3)]
        q_gain, k_gain = qkg_ref[h:h + 1, :], qkg_ref[2 + h:3 + h, :]
        q_unit, q_inv = head_norm(proj[r, cols[0]])
        k_unit, k_inv = head_norm(proj[r, cols[1]])
        qn = (q_unit * q_gain).astype(BF16)
        kn = (k_unit * k_gain).astype(BF16)
        v = proj[r, cols[2]].astype(BF16)
        hcols = slice(h * HEAD_DIM, (h + 1) * HEAD_DIM)
        cg = cg_ref[rows, hcols]
        sc = dot_t(qn, kn) * SCALE
        e = jnp.exp(sc - jnp.max(sc, axis=1, keepdims=True))
        probs = e * (1.0 / jnp.sum(e, axis=1, keepdims=True))
        low = probs.astype(BF16)
        ctx_ref[rows, hcols] = jnp.dot(low, v, preferred_element_type=F32).astype(BF16)
        dp = dot_t(cg, v)
        qkvg[rows, cols[2]] = t_dot(low, cg).astype(BF16)
        delta = jnp.sum(probs * dp, axis=1, keepdims=True)
        dsc = (probs * (dp - delta)).astype(BF16)
        dq = jnp.dot(dsc, kn, preferred_element_type=F32) * SCALE
        dk = t_dot(dsc, qn) * SCALE
        for i, (g, unit, rstd, gain) in enumerate(((dq, q_unit, q_inv, q_gain), (dk, k_unit, k_inv, k_gain))):
            part = jnp.sum(g * unit, axis=0, keepdims=True)
            row = slice(1 + 2 * i + h, 2 + 2 * i + h)
            if img > 0:
                part = part + sms[row, :HEAD_DIM]
            sms[row, :HEAD_DIM] = part
            qkvg[rows, cols[i]] = norm_back(g * gain, unit, rstd).astype(BF16)

    def sums(img):
        r = slice(GR + img * IMG, GR + (img + 1) * IMG)
        rows = slice(img * IMG, (img + 1) * IMG)
        g = qkvg[rows, :].astype(F32)
        one = jnp.sum(g * proj[0:1, :], axis=1, keepdims=True)
        two = jnp.sum(g * proj[r, :], axis=1, keepdims=True)
        lane = lax.broadcasted_iota(jnp.int32, (IMG, 128), 1)
        both = jnp.where(lane == 0, one, jnp.where(lane == 1, two, 0.0))
        sxs[:, rows] = both.T[0:8, :]

    sx_copies = []

    def sums_send():
        for o in range(1, NB):
            sx_copies.append(send(sxs, sxr.at[m], {"dp": d, "mp": (m + o) % NB}))

    def sums_end():
        sxr[m] = sxs[...]
        for c in sx_copies:
            c.wait_recv()
        total = sxr[0]
        for k in range(1, NB):
            total = total + sxr[k]
        trans[...] = jnp.zeros_like(trans)
        trans[0:8, :] = total

    cring = {}
    cx = {}

    def term(img, plane, zz):
        b = blk(plane, zz)
        w = wv[pl.ds(pl.multiple_of(b * FB, 16), FB), :]
        return dot_t(qkvg[img * IMG:(img + 1) * IMG, :], w)

    LO, HI = slice(0, HALF), slice(HALF, IMG)
    ORDER = (4, 3, 5, 2, 6, 1, 7, 0)

    def c_plane1(img, o):
        t = term(img, 1, z + o)
        cxs[img, o] = t[LO].astype(BF16)
        cx[(img, o)] = send(cxs.at[img, o], cxr.at[img, o], xh_dev)
        plane1[img, o] = t[HI].astype(BF16)
        if o == 4:
            for i, dr_ in enumerate((1, -1)):
                part = pl.ds(i * HALF // 2, HALF // 2)
                cring[(img, 1, 1, dr_)] = send(
                    plane1.at[img, o, part], t1.at[img, i, 0, part], z_dev[dr_])

    def c_add1(img, s):
        for i, dr_ in enumerate((1, -1)):
            cring[(img, 1, s, dr_)].wait_recv()
            o = (dr_ * (4 - s)) % 8
            mine = plane1[img, o].astype(F32)
            if s == 1:
                a = slice(i * HALF // 2, (i + 1) * HALF // 2)
                b = slice((1 - i) * HALF // 2, (2 - i) * HALF // 2)
                t1[img, i, 0, b] = mine[b].astype(BF16)
                t1[img, i, 0, a] = (mine[a] + t1[img, i, 0, a].astype(F32)).astype(BF16)
            else:
                t1[img, i, s - 1] = (mine + t1[img, i, s - 1].astype(F32)).astype(BF16)
            cring[(img, 1, s + 1, dr_)] = send(t1.at[img, i, s - 1], t1.at[img, i, s], z_dev[dr_])

    def c_end1(img):
        for dr_ in (1, -1):
            cring[(img, 1, 4, dr_)].wait_recv()
        tot = plane1[img, 0].astype(F32) + t1[img, 0, 3].astype(F32) + t1[img, 1, 3].astype(F32)
        cys[img] = tot.astype(BF16)
        cx[(img, "y")] = send(cys.at[img], cyr.at[img], xh_dev)

    def c_start0(img):
        t = term(img, 0, z + 4)
        cx[(img, 4)].wait_recv()
        ci[img, HALF:] = t[HI].astype(BF16)
        ci[img, :HALF] = (t[LO] + cxr[img, 4].astype(F32)).astype(BF16)
        for i, dr_ in enumerate((1, -1)):
            part = pl.ds(i * HALF, HALF)
            cring[(img, 0, 1, dr_)] = send(ci.at[img, part], cr.at[img, i, 0, part], z_dev[dr_])

    def c_add0(img, s):
        for i, dr_ in enumerate((1, -1)):
            o = (dr_ * (4 - s)) % 8
            t = term(img, 0, z + o)
            cx[(img, o)].wait_recv()
            cring[(img, 0, s, dr_)].wait_recv()
            lo = t[LO] + cxr[img, o].astype(F32)
            hi = t[HI]
            if s > 1 or i == 0:
                lo = lo + cr[img, i, s - 1, LO].astype(F32)
            if s > 1 or i == 1:
                hi = hi + cr[img, i, s - 1, HI].astype(F32)
            cr[img, i, s - 1, LO] = lo.astype(BF16)
            cr[img, i, s - 1, HI] = hi.astype(BF16)
            cring[(img, 0, s + 1, dr_)] = send(cr.at[img, i, s - 1], cr.at[img, i, s], z_dev[dr_])

    def c_final(img):
        t = term(img, 0, z)
        cx[(img, 0)].wait_recv()
        for dr_ in (1, -1):
            cring[(img, 0, 4, dr_)].wait_recv()
        cx[(img, "y")].wait_recv()
        ring_sum = cr[img, 0, 3].astype(F32) + cr[img, 1, 3].astype(F32)
        t = t + ring_sum
        lo = t[LO] + cxr[img, 0].astype(F32)
        hi = t[HI] + cyr[img].astype(F32)
        cols = trans[:, img * IMG:(img + 1) * IMG].T
        g = gain_ref[...].astype(F32)
        part = 0.0
        for j, ng in enumerate((lo, hi)):
            r = slice(GR + img * IMG + j * HALF, GR + img * IMG + (j + 1) * HALF)
            c = slice(j * HALF, (j + 1) * HALF)
            rstd = inv[r, :]
            unit = (xg[m, r, :].astype(F32) - mu[r, :]) * rstd
            part = part + jnp.sum(ng * unit, axis=0, keepdims=True)
            back = ng * g
            res = rstd * (back - cols[c, 0:1] / D - unit * (cols[c, 1:2] / D))
            ig_ref[img * IMG + j * HALF:img * IMG + (j + 1) * HALF, :] = res.astype(BF16)
        if img > 0:
            part = part + sms[0:1, :]
        sms[0:1, :] = part

    dcore, dx, dy = {}, {}, {}

    def dest(a, b, same_core):
        xl_ = xl if a == 0 else 1 - xl
        return xl_ * 8 + ((y + b) % 4) * 2 + (core if same_core else 1 - core)

    def wgrad(a, b, same_core):
        k = dest(a, b, same_core)
        return jnp.dot(nrm_t[pl.ds(pl.multiple_of(k * FB, 16), FB), :], qkvg[...], preferred_element_type=F32)

    def d_core(a, b):
        j = a * 4 + b
        ds[j] = wgrad(a, b, False).astype(BF16)
        dcore[j] = send(ds.at[j], dr.at[j], core_dev)

    XS, YS = pl.ds(0, XC), pl.ds(XC, HC - XC)

    def y_start(key, ref, cols):
        for i, dr_ in enumerate((1, -1)):
            part = pl.ds(i * FB // 2, FB // 2)
            dy[(key, 1, dr_)] = send(ref.at[part, cols], dyr.at[key, i, 0, part], y_dev[dr_])

    def d_own1(b):
        g = wgrad(1, b, True)
        j = 4 + b
        dcore[j].wait_recv()
        dr[j] = (g + dr[j].astype(F32)).astype(BF16)
        dx[b] = send(dr.at[j, :, XS], dxr.at[b], xl_dev)
        if b == 2:
            y_start(1, dr.at[j], YS)

    def d_own0(b):
        g = wgrad(0, b, True)
        dcore[b].wait_recv()
        tot = g + dr[b].astype(F32)
        dx[b].wait_recv()
        dr[b, :, XC:] = tot[:, XC:].astype(BF16)
        dr[b, :, :XC] = (tot[:, :XC] + dxr[b].astype(F32)).astype(BF16)
        if b == 2:
            y_start(2, dr.at[b], YS)
            y_start(0, dr.at[b], XS)

    def d_mid(key):
        cols = slice(0, XC) if key == 0 else slice(XC, HC)
        cds = XS if key == 0 else YS
        for i, dr_ in enumerate((1, -1)):
            j = (4 if key == 1 else 0) + (1 if i == 0 else 3)
            dy[(key, 1, dr_)].wait_recv()
            part = slice(i * FB // 2, (i + 1) * FB // 2)
            dr[j, part, cols] = (dr[j, part, cols].astype(F32) + dyr[key, i, 0, part].astype(F32)).astype(BF16)
            dy[(key, 2, dr_)] = send(dr.at[j, :, cds], dyr.at[key, i, 1], y_dev[dr_])

    def d_last(key):
        cols = slice(0, XC) if key == 0 else slice(XC, HC)
        for dr_ in (1, -1):
            dy[(key, 2, dr_)].wait_recv()
        j = 4 if key == 1 else 0
        tot = dr[j, :, cols].astype(F32) + dyr[key, 0, 1].astype(F32) + dyr[key, 1, 1].astype(F32)
        if key == 1:
            dr[j, :, cols] = tot.astype(BF16)
            dx["l"] = send(dr.at[j, :, cds_y], dxl, xl_dev)
        elif key == 0:
            wg_ref[:, cols] = tot.astype(BF16)
        else:
            dx["l"].wait_recv()
            wg_ref[:, cols] = (tot + dxl[...].astype(F32)).astype(BF16)

    cds_y = YS

    ag0(0)
    ag0(1)
    ag1(0)
    ag1(1)
    weights.wait()
    for s in (1, 2, 3, 4):
        for img in (0, 1):
            for plane in (0, 1):
                ag_hop(img, plane, s)
    ag_end(0)
    sms[...] = jnp.zeros_like(sms)
    norm(0)
    project(0)
    ag_end(1)
    attend(0, 0)
    attend(0, 1)
    sums(0)
    for o in ORDER:
        c_plane1(0, o)
    c_start0(0)
    norm(1)
    project(1)
    c_add1(0, 1)
    c_add0(0, 1)
    attend(1, 0)
    c_add1(0, 2)
    c_add0(0, 2)
    attend(1, 1)
    sums(1)
    sums_send()
    c_add1(0, 3)
    c_add0(0, 3)
    for o in ORDER:
        c_plane1(1, o)
    c_start0(1)
    transpose(0)
    transpose(1)
    for a in (1, 0):
        for b in (2, 1, 3, 0):
            d_core(a, b)
    c_end1(0)
    for b in (2, 1, 3, 0):
        d_own1(b)
    c_add1(1, 1)
    c_add0(1, 1)
    sums_end()
    c_final(0)
    d_own0(2)
    d_mid(1)
    d_own0(1)
    d_own0(3)
    d_own0(0)
    c_add1(1, 2)
    c_add0(1, 2)
    d_last(1)
    d_mid(2)
    d_mid(0)
    c_add1(1, 3)
    c_add0(1, 3)
    d_last(0)
    c_end1(1)
    c_final(1)
    sm_copies = []
    for o in range(1, NB):
        sm_copies.append(send(sms, smr.at[d], {"dp": (d + o) % NB, "mp": m}))
    smr[d] = sms[...]
    d_last(2)
    for c in sm_copies:
        c.wait_recv()
    total = smr[0]
    for k in range(1, NB):
        total = total + smr[k]
    small_ref[...] = total
    for c in sends:
        c.wait_send()


def per_device(patches, norm_gain, qkv_weight, qk_gain, context_grad):
    vmem = pl.BlockSpec(memory_space=pltpu.VMEM)
    hbm = pl.BlockSpec(memory_space=pl.ANY)
    flops = 2 * TOK * D * HC * 3
    ctx, ig, wg, small = pl.pallas_call(
        kernel,
        out_shape=(
            jax.ShapeDtypeStruct((TOK, 256), BF16),
            jax.ShapeDtypeStruct((TOK, FB), BF16),
            jax.ShapeDtypeStruct((FB, HC), BF16),
            jax.ShapeDtypeStruct((8, FB), F32),
        ),
        in_specs=[hbm, vmem, hbm, vmem, vmem],
        out_specs=(vmem, vmem, vmem, vmem),
        scratch_shapes=[
            pltpu.VMEM((NB, ROWS, FB), BF16),
            pltpu.VMEM((D, HC), BF16),
            pltpu.VMEM((ROWS, D), BF16),
            pltpu.VMEM((D, TOK), BF16),
            pltpu.VMEM((ROWS, HC), F32),
            pltpu.VMEM((TOK, HC), BF16),
            pltpu.VMEM((ROWS, 1), F32),
            pltpu.VMEM((ROWS, 1), F32),
            pltpu.VMEM((NIMG, 2, 4, IMG, FB), BF16),
            pltpu.VMEM((NIMG, IMG, FB), BF16),
            pltpu.VMEM((NIMG, 2, 4, HALF, FB), BF16),
            pltpu.VMEM((NIMG, 8, HALF, FB), BF16),
            pltpu.VMEM((NIMG, 8, HALF, FB), BF16),
            pltpu.VMEM((NIMG, HALF, FB), BF16),
            pltpu.VMEM((NIMG, HALF, FB), BF16),
            pltpu.VMEM((NIMG, 8, HALF, FB), BF16),
            pltpu.VMEM((8, FB, HC), BF16),
            pltpu.VMEM((8, FB, HC), BF16),
            pltpu.VMEM((4, FB, XC), BF16),
            pltpu.VMEM((FB, HC - XC), BF16),
            pltpu.VMEM((3, 2, 2, FB, XC), BF16),
            pltpu.VMEM((8, TOK), F32),
            pltpu.VMEM((NB, 8, TOK), F32),
            pltpu.VMEM((128, TOK), F32),
            pltpu.VMEM((8, FB), F32),
            pltpu.VMEM((NB, 8, FB), F32),
            pltpu.SemaphoreType.DMA((NSEM,)),
            pltpu.SemaphoreType.DMA((NSEM,)),
            pltpu.SemaphoreType.DMA((2,)),
        ],
        compiler_params=pltpu.CompilerParams(
            collective_id=0, has_side_effects=True, vmem_limit_bytes=62 * 2**20
        ),
        cost_estimate=pl.CostEstimate(flops=flops, bytes_accessed=2**25, transcendentals=2**18),
    )(patches, norm_gain.reshape(1, FB), qkv_weight, qk_gain.reshape(4, HEAD_DIM), context_grad)
    return ctx, ig, wg, small[0], small[1:5, :HEAD_DIM].reshape(2, 2, HEAD_DIM)


def solution(mesh):
    in_specs = (P("dp", "mp"), P("mp"), P(None, "mp"), P(None, "mp", None), P("dp", "mp"))
    out_specs = (P("dp", "mp"), P("dp", "mp"), P("dp", "mp"), P("mp"), P(None, "mp", None))
    return jax.shard_map(
        per_device, mesh=mesh, in_specs=in_specs, out_specs=out_specs, check_vma=False
    )
```

time: 594 us -> 179 us (0.30)
  waiting for transfers between devices: 380 us -> 0 us
  Pallas kernels: 0 us -> 169 us
  blocking collectives: 132 us -> 0 us
  matrix products: 38.4 us -> 0 us
  between operations: 14 us -> 0.64 us
  other arithmetic: 12.9 us -> 0 us
    unnamed x4 -> x0, waiting for transfers between devices: 201 us -> none
    pallas_call x0 -> x1, Pallas kernels: none -> 169 us  [per_device(): pl.pallas_call(kernel, out_shape=(jax.ShapeDtypeStruct((TOK, 256), BF16),...]
    psum x4 -> x0, blocking collectives: 132 us -> none  [the longest x1 38.5 us: per_device(): row_mean = lax.psum(jnp.sum(row_vals, axis=1), 'mp')[:, None] / full_width]
    all_gather x1 -> x0, waiting for transfers between devices: 131 us -> none  [per_device(): piece = lax.all_gather(normed, 'mp', axis=1, tiled=True)]
    reduce_scatter x1 -> x0, waiting for transfers between devices: 47.8 us -> none  [per_device(): lax.psum_scatter(lax.dot_general(piece, qkv_grad, (((0,), (0,)), ((), ())...]
    dot_general x8 -> x0, matrix products: 37.9 us -> none  [the longest x1 11.9 us: per_device(): lax.dot_general(piece, qkv_grad, (((0,), (0,)), ((), ())), preferred_elem...]
    convert_element_type x6 -> x0, other arithmetic: 6.77 us -> none  [the longest x1 2.14 us: per_device(): weight_grad.astype(jnp.bfloat16)]
  transfers between devices with their start and end apart: 3 -> 0, of which waited for: 3 -> 0; matrix products, arithmetic and copies ran while one was open for 3% -> 0% of each run, Pallas kernels for 0% -> 0%
where the time goes in v1:
time: 179 us
  Pallas kernels  169 us (94%)
  local copies, waits for them, and re-layouts  9.17 us (5%)
    pallas_call x1, Pallas kernels, per_device(): pl.pallas_call(kernel, out_shape=(jax.ShapeDtypeStruct((TOK, 256), BF16),...  169 us
    unnamed x3, local copies, waits for them, and re-layouts  5.36 us

profile of v1, /device:TPU:1, one launch (start us, length us, event | category | flops | bytes accessed | tf_op | source)
XLA Modules:
  0.0 178.8 jit_solution(6488476978972061091)
XLA Ops:
  0.6 1.2 reshape.19.gain_ref
  1.9 169.0 %shard_map.92 = (bf16[512,256]{1,0:T(8,128)(2,1)}, bf16[512,384]{1,0:T(8,128)(2,1)}, bf16[384,768]{1,0:T(8,128)(2,1)}, f32[8,384]{1,0:T(8,128)}) custom-call(bf16[512,384]{1,0:T(8,128)(2,1)} %p_hbm.1, bf16[1,384]{1,0:T(2,128)(2,1)} %reshape.19.gain_ref, bf16[6144,768]{1,0:T(8,128)(2,1)} %w_hbm.1, f32[4,128]{1,0:T(4,128)} %bitcast.3, bf16[512,256]{1,0:T(8,128)(2,1)} %cg_ref.1), custom_call_target="tpu_custom_call" | custom-call | flops 14495514624 | bytes 33554432 | tf_op jit(solution)/shard_map/pallas_call | solution.py:511
  170.9 1.3 slice.7
  172.2 1.3 slice_reduce_fusion
  173.5 1.7 copy.13
  175.1 1.8 copy.14
  176.9 1.9 %copy.15 = bf16[384,768]{1,0:T(8,128)(2,1)} copy(bf16[384,768]{1,0:T(8,128)(2,1)} %get-tuple-element.20) | data formatting | bytes 1179648

commit v2 on v1

v2 whole, which is shorter than its diff:
```python
import functools
import math

import jax
import jax.numpy as jnp
from jax import lax
from jax.experimental import pallas as pl
from jax.experimental.pallas import tpu as pltpu
from jax.sharding import PartitionSpec as P

HEAD_DIM = 128
IMG = 256
NIMG = 2
TOK = IMG * NIMG
FB = 384
NB = 16
D = FB * NB
HC = 768
GR = 16
ROWS = GR + TOK
HALF = IMG // 2
BASE = (0, IMG + GR)
XC = 256
LOW = (128, 64)
EPS = 1e-6
SCALE = 1.0 / math.sqrt(HEAD_DIM)
MESH = pl.DeviceIdType.MESH
F32 = jnp.float32
BF16 = jnp.bfloat16
NSEM = 192


def dot_t(a, b):
    return lax.dot_general(a, b, (((1,), (1,)), ((), ())), preferred_element_type=F32)


def t_dot(a, b):
    return lax.dot_general(a, b, (((0,), (0,)), ((), ())), preferred_element_type=F32)


def kernel(
    p_hbm, gain_ref, w_hbm, qkg_ref, cg_ref,
    ctx_ref, ig_ref, wg_ref, small_ref,
    xg, wv, nrm, nrm_t, proj, qkvg, mu, inv,
    cr, ci, ci1, t1, cxs_a, cxs_b, cxr_a, cxr_b, plane1_a, plane1_b, cys, cyr,
    ds, dr, dxr, dxl, dyx, dyy,
    sxs, sxr, trans, sms, smr,
    ss, rs, ls,
):
    d = lax.axis_index("dp")
    m = lax.axis_index("mp")
    xl, y, core = d // 8, (d // 2) % 4, d % 2
    xh, z = m // 8, m % 8
    count = [0]
    sends = []

    def at(xl_=None, y_=None, core_=None, xh_=None, z_=None):
        xl_ = xl if xl_ is None else xl_
        y_ = y if y_ is None else y_
        core_ = core if core_ is None else core_
        xh_ = xh if xh_ is None else xh_
        z_ = z if z_ is None else z_
        return {"dp": xl_ * 8 + y_ * 2 + core_, "mp": xh_ * 8 + z_}

    z_dev = {1: at(z_=(z + 1) % 8), -1: at(z_=(z + 7) % 8)}
    y_dev = {1: at(y_=(y + 1) % 4), -1: at(y_=(y + 3) % 4)}
    xh_dev = at(xh_=1 - xh)
    xl_dev = at(xl_=1 - xl)
    core_dev = at(core_=1 - core)

    def send(src, dst, dev):
        i = count[0]
        count[0] += 1
        copy = pltpu.make_async_remote_copy(
            src_ref=src, dst_ref=dst, send_sem=ss.at[i], recv_sem=rs.at[i],
            device_id=dev, device_id_type=MESH,
        )
        copy.start()
        sends.append(copy)
        return copy

    own = [
        pltpu.make_async_copy(
            p_hbm.at[pl.ds(i * IMG, IMG)], xg.at[m, pl.ds(BASE[i], IMG)], ls.at[i])
        for i in range(NIMG)
    ]
    for c in own:
        c.start()
    weights = pltpu.make_async_copy(w_hbm, wv, ls.at[2])
    weights.start()
    gain = gain_ref[...].reshape(1, FB)
    xg[m, pl.ds(IMG, GR), :] = jnp.broadcast_to(gain, (GR, FB))
    barrier = pltpu.get_barrier_semaphore()
    for o in range(1, NB):
        pl.semaphore_signal(barrier, inc=1, device_id={"dp": d, "mp": (m + o) % NB}, device_id_type=MESH)
        pl.semaphore_signal(barrier, inc=1, device_id={"dp": (d + o) % NB, "mp": m}, device_id_type=MESH)
    pl.semaphore_wait(barrier, 2 * (NB - 1))
    for c in own:
        c.wait()

    def blk(plane, zz):
        return (xh if plane == 0 else 1 - xh) * 8 + (zz + 16) % 8

    def span(img, part):
        lo0 = BASE[img]
        mid = lo0 + HALF
        end = lo0 + IMG + (GR if img == 0 else 0)
        return {
            "full": (lo0, end - lo0),
            "lo": (lo0, mid - lo0),
            "hi": (mid, end - mid),
            "hi0": (mid, HALF // 2),
            "hi1": (mid + HALF // 2, end - mid - HALF // 2),
        }[part]

    ring = {}
    xrecv = {0: [], 1: []}

    def send_block(img, plane, origin_z, part, dev):
        r, n = span(img, part)
        ref = xg.at[blk(plane, origin_z), pl.ds(r, n)]
        return send(ref, ref, dev)

    def hop_parts(plane):
        if plane == 0:
            return {1: "full", -1: "full"}, {1: "lo", -1: "hi"}
        return {1: "hi", -1: "hi"}, {1: "hi0", -1: "hi1"}

    def forward(img, plane, s):
        parts = hop_parts(plane)[0 if s < 4 else 1]
        for dr_ in (1, -1):
            ring[(img, plane, s, dr_)] = send_block(img, plane, z - (s - 1) * dr_, parts[dr_], z_dev[dr_])

    def arrive(img, plane, s):
        for dr_ in (1, -1):
            ring[(img, plane, s, dr_)].wait_recv()

    def ag0(img):
        ring[(img, "x")] = send_block(img, 0, z, "hi", xh_dev)
        forward(img, 0, 1)
        xrecv[img].append(send_block(img, 0, z, "lo", xh_dev))

    def ag1(img):
        ring[(img, "x")].wait_recv()
        forward(img, 1, 1)

    def ag_hop(img, plane, s):
        arrive(img, plane, s)
        if s < 4:
            forward(img, plane, s + 1)
        if plane == 0:
            for dr_ in (1, -1) if s < 4 else (1,):
                xrecv[img].append(send_block(img, 0, z - s * dr_, "lo", xh_dev))

    def ag_end(img):
        for c in xrecv[img]:
            c.wait_recv()

    def norm(img, half):
        @pl.loop(0, HALF // 64)
        def _(c):
            r = pl.ds(pl.multiple_of(BASE[img] + half * HALF + c * 64, 16), 64)
            shift = jnp.mean(xg[0, r, :].astype(F32), axis=1, keepdims=True)

            def stat(k, carry):
                v = xg[k, r, :].astype(F32) - shift
                w = v * v
                fold = lambda t: t[:, :128] + t[:, 128:256] + t[:, 256:]
                return carry[0] + fold(v), carry[1] + fold(w)

            zero = jnp.zeros((64, 128), F32)
            s1, s2 = lax.fori_loop(0, NB, stat, (zero, zero))
            off = jnp.sum(s1, axis=1, keepdims=True) / D
            var = jnp.sum(s2, axis=1, keepdims=True) / D - off * off
            mean = shift + off
            rstd = lax.rsqrt(jnp.maximum(var, 0.0) + EPS)
            mu[r, :] = mean
            inv[r, :] = rstd

            def put(k, _):
                g = xg[k, pl.ds(IMG, 1), :].astype(F32)
                unit = (xg[k, r, :].astype(F32) - mean) * rstd
                nrm[r, pl.ds(pl.multiple_of(k * FB, 128), FB)] = (unit * g).astype(BF16)
                return 0

            lax.fori_loop(0, NB, put, 0)

        if img == 0 and half == 1:
            @pl.loop(0, NB)
            def _(k):
                nrm[pl.ds(IMG, GR), pl.ds(pl.multiple_of(k * FB, 128), FB)] = xg[k, pl.ds(IMG, GR), :]

    def project(img):
        r = slice(0, BASE[1]) if img == 0 else slice(BASE[1], ROWS)

        @pl.loop(0, HC // 256)
        def _(c):
            cols = pl.ds(pl.multiple_of(c * 256, 256), 256)
            proj[r, cols] = jnp.dot(nrm[r, :], wv[:, cols], preferred_element_type=F32)

    def transpose(img):
        @pl.loop(0, NB)
        def _(k):
            cols = pl.ds(pl.multiple_of(k * FB, 128), FB)
            rows = slice(BASE[img], BASE[img] + IMG)
            nrm_t[cols, img * IMG:(img + 1) * IMG] = nrm[rows, cols].T

    def head_norm(v):
        cen = v - jnp.mean(v, axis=1, keepdims=True)
        rstd = lax.rsqrt(jnp.mean(cen * cen, axis=1, keepdims=True) + EPS)
        return cen * rstd, rstd

    def norm_back(g, unit, rstd):
        return rstd * (
            g - jnp.mean(g, axis=1, keepdims=True) - unit * jnp.mean(g * unit, axis=1, keepdims=True)
        )

    def attend(img, h):
        r = slice(BASE[img], BASE[img] + IMG)
        rows = slice(img * IMG, (img + 1) * IMG)
        c0 = h * 3 * HEAD_DIM
        cols = [slice(c0 + i * HEAD_DIM, c0 + (i + 1) * HEAD_DIM) for i in range(3)]
        q_gain, k_gain = qkg_ref[0, h:h + 1, :], qkg_ref[1, h:h + 1, :]
        q_unit, q_inv = head_norm(proj[r, cols[0]])
        k_unit, k_inv = head_norm(proj[r, cols[1]])
        qn = (q_unit * q_gain).astype(BF16)
        kn = (k_unit * k_gain).astype(BF16)
        v = proj[r, cols[2]].astype(BF16)
        hcols = slice(h * HEAD_DIM, (h + 1) * HEAD_DIM)
        cg = cg_ref[rows, hcols]
        sc = dot_t(qn, kn) * SCALE
        e = jnp.exp(sc - jnp.max(sc, axis=1, keepdims=True))
        probs = e * (1.0 / jnp.sum(e, axis=1, keepdims=True))
        low = probs.astype(BF16)
        ctx_ref[rows, hcols] = jnp.dot(low, v, preferred_element_type=F32).astype(BF16)
        dp = dot_t(cg, v)
        qkvg[rows, cols[2]] = t_dot(low, cg).astype(BF16)
        delta = jnp.sum(probs * dp, axis=1, keepdims=True)
        dsc = (probs * (dp - delta)).astype(BF16)
        dq = jnp.dot(dsc, kn, preferred_element_type=F32) * SCALE
        dk = t_dot(dsc, qn) * SCALE
        for i, (g, unit, rstd, gain) in enumerate(((dq, q_unit, q_inv, q_gain), (dk, k_unit, k_inv, k_gain))):
            part = jnp.sum(g * unit, axis=0, keepdims=True)
            row = slice(3 + 2 * i + h, 4 + 2 * i + h)
            if img > 0:
                part = part + sms[row, :]
            sms[row, :] = part
            qkvg[rows, cols[i]] = norm_back(g * gain, unit, rstd).astype(BF16)

    def sums(img):
        r = slice(BASE[img], BASE[img] + IMG)
        rows = slice(img * IMG, (img + 1) * IMG)
        g = qkvg[rows, :].astype(F32)
        one = jnp.sum(g * proj[IMG:IMG + 1, :], axis=1, keepdims=True)
        two = jnp.sum(g * proj[r, :], axis=1, keepdims=True)
        lane = lax.broadcasted_iota(jnp.int32, (IMG, 128), 1)
        both = jnp.where(lane == 0, one, jnp.where(lane == 1, two, 0.0))
        turned = both.T
        for i in range(2):
            for j in range(2):
                row = img * 4 + i * 2 + j
                sxs[row:row + 1, :] = turned[i:i + 1, j * 128:(j + 1) * 128]

    sx_copies = []

    def sums_send():
        for o in range(1, NB):
            sx_copies.append(send(sxs, sxr.at[m], {"dp": d, "mp": (m + o) % NB}))

    def sums_end():
        sxr[m] = sxs[...]
        for c in sx_copies:
            c.wait_recv()
        total = sxr[0]
        for k in range(1, NB):
            total = total + sxr[k]
        trans[...] = jnp.zeros_like(trans)
        for row in range(8):
            i, c = (row // 2) % 2, (row // 4) * IMG + (row % 2) * 128
            trans[i:i + 1, c:c + 128] = total[row:row + 1, :]

    cring = {}
    cx = {}

    def term(img, plane, zz):
        b = blk(plane, zz)
        w = wv[pl.ds(pl.multiple_of(b * FB, 16), FB), :]
        return dot_t(qkvg[img * IMG:(img + 1) * IMG, :], w)

    cxs, cxr, plane1 = (cxs_a, cxs_b), (cxr_a, cxr_b), (plane1_a, plane1_b)
    ORDER = (4, 3, 5, 2, 6, 1, 7, 0)

    def c_plane1(img, o):
        n = LOW[img]
        t = term(img, 1, z + o)
        cxs[img][o] = t[:n].astype(BF16)
        cx[(img, o)] = send(cxs[img].at[o], cxr[img].at[o], xh_dev)
        plane1[img][o] = t[n:].astype(BF16)

    def high(img, o):
        return plane1[img][o].astype(F32) if LOW[img] else term(img, 1, z + o)

    def c_start1(img):
        n = IMG - LOW[img]
        ci1[img, :n] = high(img, 4).astype(BF16)
        for i, dr_ in enumerate((1, -1)):
            part = pl.ds(i * n // 2, n // 2)
            cring[(img, 1, 1, dr_)] = send(ci1.at[img, part], t1.at[img, i, 0, part], z_dev[dr_])

    def c_add1(img, s):
        n = IMG - LOW[img]
        rows = pl.ds(0, n)
        for i, dr_ in enumerate((1, -1)):
            mine = high(img, (dr_ * (4 - s)) % 8)
            cring[(img, 1, s, dr_)].wait_recv()
            if s == 1:
                a = slice(i * n // 2, (i + 1) * n // 2)
                b = slice((1 - i) * n // 2, (2 - i) * n // 2)
                t1[img, i, 0, b] = mine[b].astype(BF16)
                t1[img, i, 0, a] = (mine[a] + t1[img, i, 0, a].astype(F32)).astype(BF16)
            else:
                t1[img, i, s - 1, :n] = (mine + t1[img, i, s - 1, :n].astype(F32)).astype(BF16)
            cring[(img, 1, s + 1, dr_)] = send(
                t1.at[img, i, s - 1, rows], t1.at[img, i, s, rows], z_dev[dr_])

    def c_end1(img):
        n = IMG - LOW[img]
        mine = high(img, 0)
        for dr_ in (1, -1):
            cring[(img, 1, 4, dr_)].wait_recv()
        tot = mine + t1[img, 0, 3, :n].astype(F32) + t1[img, 1, 3, :n].astype(F32)
        cys[img, :n] = tot.astype(BF16)
        cx[(img, "y")] = send(cys.at[img, pl.ds(0, n)], cyr.at[img, pl.ds(0, n)], xh_dev)

    def from_x(img, o):
        t = term(img, 0, z + o)
        n = LOW[img]
        if not n:
            return t
        cx[(img, o)].wait_recv()
        return jnp.concatenate([t[:n] + cxr[img][o].astype(F32), t[n:]], axis=0)

    def c_start0(img):
        ci[img] = from_x(img, 4).astype(BF16)
        for i, dr_ in enumerate((1, -1)):
            part = pl.ds(i * HALF, HALF)
            cring[(img, 0, 1, dr_)] = send(ci.at[img, part], cr.at[img, i, 0, part], z_dev[dr_])

    def c_add0(img, s):
        for i, dr_ in enumerate((1, -1)):
            t = from_x(img, (dr_ * (4 - s)) % 8)
            cring[(img, 0, s, dr_)].wait_recv()
            if s == 1:
                a, b = slice(i * HALF, (i + 1) * HALF), slice((1 - i) * HALF, (2 - i) * HALF)
                cr[img, i, 0, b] = t[b].astype(BF16)
                cr[img, i, 0, a] = (t[a] + cr[img, i, 0, a].astype(F32)).astype(BF16)
            else:
                cr[img, i, s - 1] = (t + cr[img, i, s - 1].astype(F32)).astype(BF16)
            cring[(img, 0, s + 1, dr_)] = send(cr.at[img, i, s - 1], cr.at[img, i, s], z_dev[dr_])

    def c_final(img):
        n = LOW[img]
        t = from_x(img, 0)
        for dr_ in (1, -1):
            cring[(img, 0, 4, dr_)].wait_recv()
        t = t + cr[img, 0, 3].astype(F32) + cr[img, 1, 3].astype(F32)
        cx[(img, "y")].wait_recv()
        rest = t[n:] + cyr[img, :IMG - n].astype(F32)
        ng = jnp.concatenate([t[:n], rest], axis=0) if n else rest
        cols = trans[:, img * IMG:(img + 1) * IMG].T
        r = slice(BASE[img], BASE[img] + IMG)
        rstd = inv[r, :]
        unit = (xg[m, r, :].astype(F32) - mu[r, :]) * rstd
        part = jnp.sum(ng * unit, axis=0, keepdims=True)
        back = ng * gain.astype(F32)
        res = rstd * (back - cols[:, 0:1] / D - unit * (cols[:, 1:2] / D))
        ig_ref[img * IMG:(img + 1) * IMG, :] = res.astype(BF16)
        for i in range(3):
            sms[i:i + 1, :] = sms[i:i + 1, :] + part[:, i * 128:(i + 1) * 128]

    dcore, dx, dy = {}, {}, {}

    def dest(a, b, same_core):
        xl_ = xl if a == 0 else 1 - xl
        return xl_ * 8 + ((y + b) % 4) * 2 + (core if same_core else 1 - core)

    def wgrad(a, b, same_core):
        k = dest(a, b, same_core)
        return jnp.dot(nrm_t[pl.ds(pl.multiple_of(k * FB, 16), FB), :], qkvg[...], preferred_element_type=F32)

    def d_core(a, b):
        j = a * 4 + b
        ds[j] = wgrad(a, b, False).astype(BF16)
        dcore[j] = send(ds.at[j], dr.at[j], core_dev)

    XS, YS = pl.ds(0, XC), pl.ds(XC, HC - XC)

    def y_buf(key):
        return dyx if key == 0 else dyy.at[key - 1]

    def y_start(key, ref, cols):
        for i, dr_ in enumerate((1, -1)):
            part = pl.ds(i * FB // 2, FB // 2)
            dy[(key, 1, dr_)] = send(ref.at[part, cols], y_buf(key).at[i, 0, part], y_dev[dr_])

    def d_own1(b):
        g = wgrad(1, b, True)
        j = 4 + b
        dcore[j].wait_recv()
        dr[j] = (g + dr[j].astype(F32)).astype(BF16)
        dx[b] = send(dr.at[j, :, XS], dxr.at[b], xl_dev)
        if b == 2:
            y_start(1, dr.at[j], YS)

    def d_own0(b):
        g = wgrad(0, b, True)
        dcore[b].wait_recv()
        dr[b] = (g + dr[b].astype(F32)).astype(BF16)
        if b == 2:
            y_start(2, dr.at[b], YS)

    def d_x0(b):
        dx[b].wait_recv()
        dr[b, :, :XC] = (dr[b, :, :XC].astype(F32) + dxr[b].astype(F32)).astype(BF16)
        if b == 2:
            y_start(0, dr.at[b], XS)

    def d_mid(key):
        cols = slice(0, XC) if key == 0 else slice(XC, HC)
        cds = XS if key == 0 else YS
        buf = y_buf(key)
        for i, dr_ in enumerate((1, -1)):
            j = (4 if key == 1 else 0) + (1 if i == 0 else 3)
            dy[(key, 1, dr_)].wait_recv()
            part = slice(i * FB // 2, (i + 1) * FB // 2)
            dr[j, part, cols] = (dr[j, part, cols].astype(F32) + buf[i, 0, part].astype(F32)).astype(BF16)
            dy[(key, 2, dr_)] = send(dr.at[j, :, cds], buf.at[i, 1], y_dev[dr_])

    def d_last(key):
        cols = slice(0, XC) if key == 0 else slice(XC, HC)
        buf = y_buf(key)
        for dr_ in (1, -1):
            dy[(key, 2, dr_)].wait_recv()
        j = 4 if key == 1 else 0
        tot = dr[j, :, cols].astype(F32) + buf[0, 1].astype(F32) + buf[1, 1].astype(F32)
        if key == 1:
            dr[j, :, cols] = tot.astype(BF16)
            dx["l"] = send(dr.at[j, :, YS], dxl, xl_dev)
        elif key == 0:
            wg_ref[:, cols] = tot.astype(BF16)
        else:
            dx["l"].wait_recv()
            wg_ref[:, cols] = (tot + dxl[...].astype(F32)).astype(BF16)

    def sums_start():
        sms[...] = jnp.zeros_like(sms)

    def small_send():
        for o in range(1, NB):
            sm_copies.append(send(sms, smr.at[d], {"dp": (d + o) % NB, "mp": m}))
        smr[d] = sms[...]

    def small_end():
        for c in sm_copies:
            c.wait_recv()
        total = smr[0]
        for k in range(1, NB):
            total = total + smr[k]
        small_ref[...] = total

    sm_copies = []
    steps = []

    def do(f, *a):
        steps.append((f, a))

    do(ag0, 0)
    do(ag0, 1)
    do(weights.wait)
    do(ag_hop, 0, 0, 1)
    do(sums_start)
    do(ag1, 0)
    do(ag_hop, 0, 0, 2)
    do(ag_hop, 0, 1, 1)
    do(ag_hop, 0, 0, 3)
    do(ag_hop, 0, 1, 2)
    do(ag_hop, 1, 0, 1)
    do(ag_hop, 0, 1, 3)
    do(ag1, 1)
    do(ag_hop, 0, 0, 4)
    do(ag_hop, 1, 0, 2)
    do(ag_hop, 0, 1, 4)
    do(norm, 0, 1)
    do(ag_hop, 1, 1, 1)
    do(ag_end, 0)
    do(norm, 0, 0)
    do(project, 0)
    do(ag_hop, 1, 0, 3)
    do(attend, 0, 0)
    do(ag_hop, 1, 1, 2)
    do(attend, 0, 1)
    do(c_plane1, 0, 4)
    do(c_start1, 0)
    do(ag_hop, 1, 0, 4)
    do(c_plane1, 0, 5)
    do(transpose, 0)
    do(ag_hop, 1, 1, 3)
    do(sums, 0)
    do(c_plane1, 0, 3)
    do(c_add1, 0, 1)
    do(c_plane1, 0, 7)
    do(c_plane1, 0, 1)
    do(c_plane1, 0, 6)
    do(c_start0, 0)
    do(ag_hop, 1, 1, 4)
    do(norm, 1, 1)
    do(c_plane1, 0, 2)
    do(c_add1, 0, 2)
    do(ag_end, 1)
    do(norm, 1, 0)
    do(project, 1)
    do(c_add1, 0, 3)
    do(c_add0, 0, 1)
    do(attend, 1, 0)
    do(attend, 1, 1)
    do(c_plane1, 1, 4)
    do(c_start1, 1)
    do(sums, 1)
    do(c_plane1, 1, 5)
    do(c_plane1, 1, 0)
    do(transpose, 1)
    do(d_core, 1, 2)
    do(c_plane1, 1, 1)
    do(sums_send)
    do(c_start0, 1)
    do(d_core, 1, 3)
    do(c_plane1, 1, 2)
    do(c_plane1, 1, 3)
    do(c_add1, 1, 1)
    do(d_own1, 2)
    do(d_core, 0, 1)
    do(d_core, 0, 2)
    do(c_add0, 0, 2)
    do(c_plane1, 1, 7)
    do(d_own1, 3)
    do(c_add0, 1, 1)
    do(d_core, 1, 1)
    do(d_own0, 2)
    do(d_x0, 2)
    do(d_core, 0, 3)
    do(c_plane1, 1, 6)
    do(d_own1, 1)
    do(d_mid, 1)
    do(c_plane1, 0, 0)
    do(d_core, 1, 0)
    do(c_add1, 1, 2)
    do(c_end1, 0)
    do(d_own0, 3)
    do(c_add0, 1, 2)
    do(sums_end)
    do(d_own1, 0)
    do(d_x0, 3)
    do(d_own0, 1)
    do(d_x0, 1)
    do(c_add1, 1, 3)
    do(d_core, 0, 0)
    do(c_add0, 0, 3)
    do(d_mid, 0)
    do(c_add0, 1, 3)
    do(d_mid, 2)
    do(c_end1, 1)
    do(d_last, 1)
    do(c_final, 0)
    do(d_own0, 0)
    do(d_x0, 0)
    do(d_last, 0)
    do(c_final, 1)
    do(small_send)
    do(small_end)
    do(d_last, 2)
    for f, a in steps:
        f(*a)
    for c in sends:
        c.wait_send()


def place(ctx, ig, wg, small, ctx_out, ig_out, wg_out, ngg_out, qkg_out):
    ctx_out[...] = ctx[...]
    ig_out[...] = ig[...]
    wg_out[...] = wg[...]
    for i in range(3):
        ngg_out[pl.ds(i * 128, 128)] = small[i, :]
    for i in range(2):
        qkg_out[i] = small[3 + 2 * i:5 + 2 * i, :]


def per_device(patches, norm_gain, qkv_weight, qk_gain, context_grad):
    vmem = pl.BlockSpec(memory_space=pltpu.VMEM)
    hbm = pl.BlockSpec(memory_space=pl.ANY)
    flops = 2 * TOK * D * HC * 3
    ctx, ig, wg, small = pl.pallas_call(
        kernel,
        out_shape=(
            jax.ShapeDtypeStruct((TOK, 256), BF16),
            jax.ShapeDtypeStruct((TOK, FB), BF16),
            jax.ShapeDtypeStruct((FB, HC), BF16),
            jax.ShapeDtypeStruct((8, 128), F32),
        ),
        in_specs=[hbm, vmem, hbm, vmem, vmem],
        out_specs=(vmem, vmem, vmem, vmem),
        scratch_shapes=[
            pltpu.VMEM((NB, ROWS, FB), BF16),
            pltpu.VMEM((D, HC), BF16),
            pltpu.VMEM((ROWS, D), BF16),
            pltpu.VMEM((D, TOK), BF16),
            pltpu.VMEM((ROWS, HC), F32),
            pltpu.VMEM((TOK, HC), BF16),
            pltpu.VMEM((ROWS, 1), F32),
            pltpu.VMEM((ROWS, 1), F32),
            pltpu.VMEM((NIMG, 2, 4, IMG, FB), BF16),
            pltpu.VMEM((NIMG, IMG, FB), BF16),
            pltpu.VMEM((NIMG, IMG, FB), BF16),
            pltpu.VMEM((NIMG, 2, 4, IMG, FB), BF16),
            *[pltpu.VMEM((8, max(n, 16), FB), BF16) for n in LOW],
            *[pltpu.VMEM((8, max(n, 16), FB), BF16) for n in LOW],
            *[pltpu.VMEM((8, IMG - n if n else 16, FB), BF16) for n in LOW],
            pltpu.VMEM((NIMG, IMG, FB), BF16),
            pltpu.VMEM((NIMG, IMG, FB), BF16),
            pltpu.VMEM((8, FB, HC), BF16),
            pltpu.VMEM((8, FB, HC), BF16),
            pltpu.VMEM((4, FB, XC), BF16),
            pltpu.VMEM((FB, HC - XC), BF16),
            pltpu.VMEM((2, 2, FB, XC), BF16),
            pltpu.VMEM((2, 2, 2, FB, HC - XC), BF16),
            pltpu.VMEM((8, 128), F32),
            pltpu.VMEM((NB, 8, 128), F32),
            pltpu.VMEM((128, TOK), F32),
            pltpu.VMEM((8, 128), F32),
            pltpu.VMEM((NB, 8, 128), F32),
            pltpu.SemaphoreType.DMA((NSEM,)),
            pltpu.SemaphoreType.DMA((NSEM,)),
            pltpu.SemaphoreType.DMA((3,)),
        ],
        compiler_params=pltpu.CompilerParams(
            collective_id=0, has_side_effects=True, vmem_limit_bytes=62 * 2**20
        ),
        cost_estimate=pl.CostEstimate(flops=flops, bytes_accessed=2**25, transcendentals=2**18),
    )(patches, norm_gain, qkv_weight, qk_gain, context_grad)
    return pl.pallas_call(
        place,
        out_shape=(
            jax.ShapeDtypeStruct((TOK, 256), BF16),
            jax.ShapeDtypeStruct((TOK, FB), BF16),
            jax.ShapeDtypeStruct((FB, HC), BF16),
            jax.ShapeDtypeStruct((FB,), F32),
            jax.ShapeDtypeStruct((2, 2, HEAD_DIM), F32),
        ),
        in_specs=[vmem] * 4,
        out_specs=(vmem,) * 5,
    )(ctx, ig, wg, small)


def solution(mesh):
    in_specs = (P("dp", "mp"), P("mp"), P(None, "mp"), P(None, "mp", None), P("dp", "mp"))
    out_specs = (P("dp", "mp"), P("dp", "mp"), P("dp", "mp"), P("mp"), P(None, "mp", None))
    return jax.shard_map(
        per_device, mesh=mesh, in_specs=in_specs, out_specs=out_specs, check_vma=False
    )
```

time: 179 us -> 130 us (0.73)
  Pallas kernels: 169 us -> 129 us
  local copies, waits for them, and re-layouts: 9.17 us -> 0 us
    pallas_call x1, Pallas kernels: 169 us -> 127 us  [per_device(): pl.pallas_call(kernel, out_shape=(jax.ShapeDtypeStruct((TOK, 256), BF16),...]
    unnamed x3 -> x0, local copies, waits for them, and re-layouts: 5.36 us -> none
    slice x2 -> x0, local copies, waits for them, and re-layouts: 2.57 us -> none  [the longest x1 1.3 us: per_device(): small[0]]
    pallas_call x0 -> x1, Pallas kernels: none -> 2.34 us  [per_device(): pl.pallas_call(place, out_shape=(jax.ShapeDtypeStruct((TOK, 256), BF16),...]
where the time goes in v2:
time: 130 us
  Pallas kernels  129 us (99%)
    pallas_call x1, Pallas kernels, per_device(): pl.pallas_call(kernel, out_shape=(jax.ShapeDtypeStruct((TOK, 256), BF16),...  127 us

profile of v2, /device:TPU:1, one launch (start us, length us, event | category | flops | bytes accessed | tf_op | source)
XLA Modules:
  0.0 129.9 jit_solution(8413029638737097935)
XLA Ops:
  0.6 127.0 %shard_map.92 = (bf16[512,256]{1,0:T(8,128)(2,1)}, bf16[512,384]{1,0:T(8,128)(2,1)}, bf16[384,768]{1,0:T(8,128)(2,1)}, f32[8,128]{1,0:T(8,128)}) custom-call(bf16[512,384]{1,0:T(8,128)(2,1)} %p_hbm.1, bf16[384]{0:T(512)(128)(2,1)} %gain_ref.1, bf16[6144,768]{1,0:T(8,128)(2,1)} %w_hbm.1, f32[2,2,128]{2,1,0:T(2,128)} %qkg_ref.1, bf16[512,256]{1,0:T(8,128)(2,1)} %cg_ref.1), custom_call_target="tpu_custom_call" | custom-call | flops 14495514624 | bytes 33554432 | tf_op jit(solution)/shard_map/pallas_call | solution.py:601
  127.6 2.3 %shard_map.93 = (bf16[512,256]{1,0:T(8,128)(2,1)}, bf16[512,384]{1,0:T(8,128)(2,1)}, bf16[384,768]{1,0:T(8,128)(2,1)}, f32[384]{0:T(512)}, f32[2,2,128]{2,1,0:T(2,128)}) custom-call(bf16[512,256]{1,0:T(8,128)(2,1)} %get-tuple-element.9.ctx, bf16[512,384]{1,0:T(8,128)(2,1)} %get-tuple-element.10.ig, bf16[384,768]{1,0:T(8,128)(2,1)} %get-tuple-element.11.wg, ...), custom_call_target="tpu_custom_call" | custom-call | tf_op jit(solution)/shard_map/pallas_call | solution.py:649

commit v3 on v2

--- a/solution.py
+++ b/solution.py
@@ -20,8 +20,8 @@
 ROWS = GR + TOK
 HALF = IMG // 2
 BASE = (0, IMG + GR)
-XC = 256
-LOW = (128, 64)
+XC = 128
+LOW = (96, 96)
 EPS = 1e-6
 SCALE = 1.0 / math.sqrt(HEAD_DIM)
 MESH = pl.DeviceIdType.MESH
@@ -39,9 +39,9 @@
 
 
 def kernel(
-    p_hbm, gain_ref, w_hbm, qkg_ref, cg_ref,
+    p_hbm, gain_hbm, w_hbm, qkg_hbm, cg_hbm,
     ctx_ref, ig_ref, wg_ref, small_ref,
-    xg, wv, nrm, nrm_t, proj, qkvg, mu, inv,
+    gain_ref, qkg_ref, cg_ref, xg, wv, nrm, nrm_t, proj, qkvg, mu, inv,
     cr, ci, ci1, t1, cxs_a, cxs_b, cxr_a, cxr_b, plane1_a, plane1_b, cys, cyr,
     ds, dr, dxr, dxl, dyx, dyy,
     sxs, sxr, trans, sms, smr,
@@ -79,6 +79,10 @@
         sends.append(copy)
         return copy
 
+    barrier = pltpu.get_barrier_semaphore()
+    near = (z_dev[1], z_dev[-1], xh_dev, y_dev[1], y_dev[-1], xl_dev, core_dev)
+    for other in near:
+        pl.semaphore_signal(barrier, inc=1, device_id=other, device_id_type=MESH)
     own = [
         pltpu.make_async_copy(
             p_hbm.at[pl.ds(i * IMG, IMG)], xg.at[m, pl.ds(BASE[i], IMG)], ls.at[i])
@@ -87,15 +91,18 @@
     for c in own:
         c.start()
     weights = pltpu.make_async_copy(w_hbm, wv, ls.at[2])
+    small_in = [
+        pltpu.make_async_copy(a, b, ls.at[3 + i])
+        for i, (a, b) in enumerate(((gain_hbm, gain_ref), (qkg_hbm, qkg_ref), (cg_hbm, cg_ref)))
+    ]
+    for c in small_in:
+        c.start()
     weights.start()
+    small_in[0].wait()
     gain = gain_ref[...].reshape(1, FB)
     xg[m, pl.ds(IMG, GR), :] = jnp.broadcast_to(gain, (GR, FB))
-    barrier = pltpu.get_barrier_semaphore()
-    for o in range(1, NB):
-        pl.semaphore_signal(barrier, inc=1, device_id={"dp": d, "mp": (m + o) % NB}, device_id_type=MESH)
-        pl.semaphore_signal(barrier, inc=1, device_id={"dp": (d + o) % NB, "mp": m}, device_id_type=MESH)
-    pl.semaphore_wait(barrier, 2 * (NB - 1))
-    for c in own:
+    pl.semaphore_wait(barrier, len(near))
+    for c in own + small_in[1:]:
         c.wait()
 
     def blk(plane, zz):
@@ -475,25 +482,25 @@
         steps.append((f, a))
 
     do(ag0, 0)
+    do(ag1, 0)
+    do(ag_hop, 0, 0, 1)
+    do(ag_hop, 0, 1, 1)
+    do(ag_hop, 0, 0, 2)
+    do(ag_hop, 0, 1, 2)
     do(ag0, 1)
-    do(weights.wait)
-    do(ag_hop, 0, 0, 1)
+    do(ag_hop, 0, 1, 3)
+    do(ag_hop, 0, 0, 3)
+    do(ag_hop, 1, 0, 1)
+    do(ag1, 1)
     do(sums_start)
-    do(ag1, 0)
-    do(ag_hop, 0, 0, 2)
-    do(ag_hop, 0, 1, 1)
-    do(ag_hop, 0, 0, 3)
-    do(ag_hop, 0, 1, 2)
-    do(ag_hop, 1, 0, 1)
-    do(ag_hop, 0, 1, 3)
-    do(ag1, 1)
+    do(ag_hop, 0, 1, 4)
     do(ag_hop, 0, 0, 4)
+    do(norm, 0, 1)
     do(ag_hop, 1, 0, 2)
-    do(ag_hop, 0, 1, 4)
-    do(norm, 0, 1)
-    do(ag_hop, 1, 1, 1)
     do(ag_end, 0)
     do(norm, 0, 0)
+    do(ag_hop, 1, 1, 1)
+    do(weights.wait)
     do(project, 0)
     do(ag_hop, 1, 0, 3)
     do(attend, 0, 0)
@@ -501,83 +508,83 @@
     do(attend, 0, 1)
     do(c_plane1, 0, 4)
     do(c_start1, 0)
+    do(transpose, 0)
     do(ag_hop, 1, 0, 4)
+    do(c_plane1, 0, 3)
     do(c_plane1, 0, 5)
-    do(transpose, 0)
     do(ag_hop, 1, 1, 3)
-    do(sums, 0)
-    do(c_plane1, 0, 3)
+    do(c_plane1, 0, 6)
+    do(c_plane1, 0, 2)
     do(c_add1, 0, 1)
+    do(c_plane1, 0, 0)
+    do(c_start0, 0)
     do(c_plane1, 0, 7)
-    do(c_plane1, 0, 1)
-    do(c_plane1, 0, 6)
-    do(c_start0, 0)
     do(ag_hop, 1, 1, 4)
     do(norm, 1, 1)
-    do(c_plane1, 0, 2)
-    do(c_add1, 0, 2)
     do(ag_end, 1)
     do(norm, 1, 0)
+    do(c_add1, 0, 2)
+    do(transpose, 1)
+    do(c_add0, 0, 1)
     do(project, 1)
-    do(c_add1, 0, 3)
-    do(c_add0, 0, 1)
     do(attend, 1, 0)
     do(attend, 1, 1)
     do(c_plane1, 1, 4)
     do(c_start1, 1)
-    do(sums, 1)
-    do(c_plane1, 1, 5)
-    do(c_plane1, 1, 0)
-    do(transpose, 1)
     do(d_core, 1, 2)
-    do(c_plane1, 1, 1)
-    do(sums_send)
-    do(c_start0, 1)
+    do(c_plane1, 0, 1)
+    do(c_add1, 0, 3)
     do(d_core, 1, 3)
-    do(c_plane1, 1, 2)
-    do(c_plane1, 1, 3)
-    do(c_add1, 1, 1)
-    do(d_own1, 2)
-    do(d_core, 0, 1)
-    do(d_core, 0, 2)
     do(c_add0, 0, 2)
     do(c_plane1, 1, 7)
-    do(d_own1, 3)
-    do(c_add0, 1, 1)
+    do(d_own1, 2)
+    do(d_core, 0, 2)
+    do(c_plane1, 1, 3)
+    do(c_plane1, 1, 5)
+    do(c_add1, 1, 1)
+    do(c_start0, 1)
+    do(c_plane1, 1, 2)
+    do(sums, 1)
+    do(c_plane1, 1, 6)
     do(d_core, 1, 1)
     do(d_own0, 2)
+    do(sums, 0)
+    do(c_end1, 0)
+    do(d_own1, 3)
+    do(d_own1, 1)
     do(d_x0, 2)
     do(d_core, 0, 3)
-    do(c_plane1, 1, 6)
-    do(d_own1, 1)
+    do(c_add1, 1, 2)
+    do(c_plane1, 1, 1)
     do(d_mid, 1)
-    do(c_plane1, 0, 0)
     do(d_core, 1, 0)
-    do(c_add1, 1, 2)
-    do(c_end1, 0)
+    do(c_add0, 1, 1)
+    do(sums_send)
+    do(d_own1, 0)
     do(d_own0, 3)
+    do(d_core, 0, 1)
+    do(c_add1, 1, 3)
+    do(d_core, 0, 0)
     do(c_add0, 1, 2)
-    do(sums_end)
-    do(d_own1, 0)
+    do(c_add0, 0, 3)
+    do(c_plane1, 1, 0)
+    do(c_end1, 1)
     do(d_x0, 3)
     do(d_own0, 1)
     do(d_x0, 1)
-    do(c_add1, 1, 3)
-    do(d_core, 0, 0)
-    do(c_add0, 0, 3)
     do(d_mid, 0)
-    do(c_add0, 1, 3)
-    do(d_mid, 2)
-    do(c_end1, 1)
-    do(d_last, 1)
-    do(c_final, 0)
     do(d_own0, 0)
     do(d_x0, 0)
+    do(d_last, 1)
+    do(d_mid, 2)
     do(d_last, 0)
+    do(c_add0, 1, 3)
+    do(sums_end)
+    do(c_final, 0)
     do(c_final, 1)
     do(small_send)
+    do(d_last, 2)
     do(small_end)
-    do(d_last, 2)
     for f, a in steps:
         f(*a)
     for c in sends:
@@ -606,9 +613,12 @@
             jax.ShapeDtypeStruct((FB, HC), BF16),
             jax.ShapeDtypeStruct((8, 128), F32),
         ),
-        in_specs=[hbm, vmem, hbm, vmem, vmem],
+        in_specs=[hbm] * 5,
         out_specs=(vmem, vmem, vmem, vmem),
         scratch_shapes=[
+            pltpu.VMEM((FB,), BF16),
+            pltpu.VMEM((2, 2, HEAD_DIM), F32),
+            pltpu.VMEM((TOK, 256), BF16),
             pltpu.VMEM((NB, ROWS, FB), BF16),
             pltpu.VMEM((D, HC), BF16),
             pltpu.VMEM((ROWS, D), BF16),
@@ -639,7 +649,7 @@
             pltpu.VMEM((NB, 8, 128), F32),
             pltpu.SemaphoreType.DMA((NSEM,)),
             pltpu.SemaphoreType.DMA((NSEM,)),
-            pltpu.SemaphoreType.DMA((3,)),
+            pltpu.SemaphoreType.DMA((6,)),
         ],
         compiler_params=pltpu.CompilerParams(
             collective_id=0, has_side_effects=True, vmem_limit_bytes=62 * 2**20

time: 130 us -> 124 us (0.954)
  Pallas kernels: 129 us -> 123 us
    pallas_call x1, Pallas kernels: 127 us -> 121 us  [per_device(): pl.pallas_call(kernel, out_shape=(jax.ShapeDtypeStruct((TOK, 256), BF16),...]
where the time goes in v3:
time: 124 us
  Pallas kernels  123 us (99%)
    pallas_call x1, Pallas kernels, per_device(): pl.pallas_call(kernel, out_shape=(jax.ShapeDtypeStruct((TOK, 256), BF16),...  121 us

profile of v3, /device:TPU:1, one launch (start us, length us, event | category | flops | bytes accessed | tf_op | source)
XLA Modules:
  0.0 123.9 jit_solution(13258496841741246935)
XLA Ops:
  0.6 120.9 %shard_map.92 = (bf16[512,256]{1,0:T(8,128)(2,1)}, bf16[512,384]{1,0:T(8,128)(2,1)}, bf16[384,768]{1,0:T(8,128)(2,1)}, f32[8,128]{1,0:T(8,128)}) custom-call(bf16[512,384]{1,0:T(8,128)(2,1)} %p_hbm.1, bf16[384]{0:T(512)(128)(2,1)} %gain_hbm.1, bf16[6144,768]{1,0:T(8,128)(2,1)} %w_hbm.1, f32[2,2,128]{2,1,0:T(2,128)} %qkg_hbm.1, bf16[512,256]{1,0:T(8,128)(2,1)} %cg_hbm.1), custom_call_target="tpu_custom_call" | custom-call | flops 14495514624 | bytes 33554432 | tf_op jit(solution)/shard_map/pallas_call | solution.py:608
  121.5 2.3 %shard_map.93 = (bf16[512,256]{1,0:T(8,128)(2,1)}, bf16[512,384]{1,0:T(8,128)(2,1)}, bf16[384,768]{1,0:T(8,128)(2,1)}, f32[384]{0:T(512)}, f32[2,2,128]{2,1,0:T(2,128)}) custom-call(bf16[512,256]{1,0:T(8,128)(2,1)} %get-tuple-element.9.ctx, bf16[512,384]{1,0:T(8,128)(2,1)} %get-tuple-element.10.ig, bf16[384,768]{1,0:T(8,128)(2,1)} %get-tuple-element.11.wg, ...), custom_call_target="tpu_custom_call" | custom-call | tf_op jit(solution)/shard_map/pallas_call | solution.py:659

commit v4 on v3

--- a/solution.py
+++ b/solution.py
@@ -21,7 +21,9 @@
 HALF = IMG // 2
 BASE = (0, IMG + GR)
 XC = 128
-LOW = (96, 96)
+MID = 384
+STREAMS = ((0, 0, XC), (1, XC, MID), (0, XC, MID), (1, MID, HC), (0, MID, HC))
+LOW = (128, 96)
 EPS = 1e-6
 SCALE = 1.0 / math.sqrt(HEAD_DIM)
 MESH = pl.DeviceIdType.MESH
@@ -40,10 +42,11 @@
 
 def kernel(
     p_hbm, gain_hbm, w_hbm, qkg_hbm, cg_hbm,
+    ctx_hbm, ig_hbm, wg_hbm, small_hbm,
     ctx_ref, ig_ref, wg_ref, small_ref,
     gain_ref, qkg_ref, cg_ref, xg, wv, nrm, nrm_t, proj, qkvg, mu, inv,
     cr, ci, ci1, t1, cxs_a, cxs_b, cxr_a, cxr_b, plane1_a, plane1_b, cys, cyr,
-    ds, dr, dxr, dxl, dyx, dyy,
+    dr, dxr, dxl_a, dxl_b, dy_a, dy_b, dy_c, dy_d, dy_e,
     sxs, sxr, trans, sms, smr,
     ss, rs, ls,
 ):
@@ -53,6 +56,12 @@
     xh, z = m // 8, m % 8
     count = [0]
     sends = []
+    outs = []
+
+    def put_out(src, dst):
+        c = pltpu.make_async_copy(src, dst, ls.at[6 + len(outs)])
+        c.start()
+        outs.append(c)
 
     def at(xl_=None, y_=None, core_=None, xh_=None, z_=None):
         xl_ = xl if xl_ is None else xl_
@@ -271,6 +280,7 @@
     sx_copies = []
 
     def sums_send():
+        put_out(ctx_ref, ctx_hbm)
         for o in range(1, NB):
             sx_copies.append(send(sxs, sxr.at[m], {"dp": d, "mp": (m + o) % NB}))
 
@@ -382,6 +392,8 @@
         back = ng * gain.astype(F32)
         res = rstd * (back - cols[:, 0:1] / D - unit * (cols[:, 1:2] / D))
         ig_ref[img * IMG:(img + 1) * IMG, :] = res.astype(BF16)
+        part_rows = pl.ds(img * IMG, IMG)
+        put_out(ig_ref.at[part_rows], ig_hbm.at[part_rows])
         for i in range(3):
             sms[i:i + 1, :] = sms[i:i + 1, :] + part[:, i * 128:(i + 1) * 128]
 
@@ -397,18 +409,19 @@
 
     def d_core(a, b):
         j = a * 4 + b
-        ds[j] = wgrad(a, b, False).astype(BF16)
-        dcore[j] = send(ds.at[j], dr.at[j], core_dev)
-
-    XS, YS = pl.ds(0, XC), pl.ds(XC, HC - XC)
-
-    def y_buf(key):
-        return dyx if key == 0 else dyy.at[key - 1]
-
-    def y_start(key, ref, cols):
+        nrm[:FB, j * HC:(j + 1) * HC] = wgrad(a, b, False).astype(BF16)
+        dcore[j] = send(nrm.at[pl.ds(0, FB), pl.ds(j * HC, HC)], dr.at[j], core_dev)
+
+    XS = pl.ds(0, XC)
+    ybuf = (dy_a, dy_b, dy_c, dy_d, dy_e)
+    dxl = {1: dxl_a, 3: dxl_b}
+
+    def y_start(key, j):
+        _, c0, c1 = STREAMS[key]
         for i, dr_ in enumerate((1, -1)):
             part = pl.ds(i * FB // 2, FB // 2)
-            dy[(key, 1, dr_)] = send(ref.at[part, cols], y_buf(key).at[i, 0, part], y_dev[dr_])
+            dy[(key, 1, dr_)] = send(
+                dr.at[j, part, pl.ds(c0, c1 - c0)], ybuf[key].at[i, 0, part], y_dev[dr_])
 
     def d_own1(b):
         g = wgrad(1, b, True)
@@ -417,47 +430,49 @@
         dr[j] = (g + dr[j].astype(F32)).astype(BF16)
         dx[b] = send(dr.at[j, :, XS], dxr.at[b], xl_dev)
         if b == 2:
-            y_start(1, dr.at[j], YS)
+            y_start(1, j)
+            y_start(3, j)
 
     def d_own0(b):
         g = wgrad(0, b, True)
         dcore[b].wait_recv()
         dr[b] = (g + dr[b].astype(F32)).astype(BF16)
         if b == 2:
-            y_start(2, dr.at[b], YS)
+            y_start(2, b)
+            y_start(4, b)
 
     def d_x0(b):
         dx[b].wait_recv()
         dr[b, :, :XC] = (dr[b, :, :XC].astype(F32) + dxr[b].astype(F32)).astype(BF16)
         if b == 2:
-            y_start(0, dr.at[b], XS)
+            y_start(0, b)
 
     def d_mid(key):
-        cols = slice(0, XC) if key == 0 else slice(XC, HC)
-        cds = XS if key == 0 else YS
-        buf = y_buf(key)
+        half, c0, c1 = STREAMS[key]
+        buf = ybuf[key]
         for i, dr_ in enumerate((1, -1)):
-            j = (4 if key == 1 else 0) + (1 if i == 0 else 3)
+            j = half * 4 + (1 if i == 0 else 3)
             dy[(key, 1, dr_)].wait_recv()
             part = slice(i * FB // 2, (i + 1) * FB // 2)
-            dr[j, part, cols] = (dr[j, part, cols].astype(F32) + buf[i, 0, part].astype(F32)).astype(BF16)
-            dy[(key, 2, dr_)] = send(dr.at[j, :, cds], buf.at[i, 1], y_dev[dr_])
+            dr[j, part, c0:c1] = (dr[j, part, c0:c1].astype(F32) + buf[i, 0, part].astype(F32)).astype(BF16)
+            dy[(key, 2, dr_)] = send(dr.at[j, :, pl.ds(c0, c1 - c0)], buf.at[i, 1], y_dev[dr_])
 
     def d_last(key):
-        cols = slice(0, XC) if key == 0 else slice(XC, HC)
-        buf = y_buf(key)
+        half, c0, c1 = STREAMS[key]
+        buf = ybuf[key]
         for dr_ in (1, -1):
             dy[(key, 2, dr_)].wait_recv()
-        j = 4 if key == 1 else 0
-        tot = dr[j, :, cols].astype(F32) + buf[0, 1].astype(F32) + buf[1, 1].astype(F32)
-        if key == 1:
-            dr[j, :, cols] = tot.astype(BF16)
-            dx["l"] = send(dr.at[j, :, YS], dxl, xl_dev)
-        elif key == 0:
-            wg_ref[:, cols] = tot.astype(BF16)
-        else:
-            dx["l"].wait_recv()
-            wg_ref[:, cols] = (tot + dxl[...].astype(F32)).astype(BF16)
+        j = half * 4
+        tot = dr[j, :, c0:c1].astype(F32) + buf[0, 1].astype(F32) + buf[1, 1].astype(F32)
+        if half == 1:
+            dr[j, :, c0:c1] = tot.astype(BF16)
+            dx[("l", key)] = send(dr.at[j, :, pl.ds(c0, c1 - c0)], dxl[key], xl_dev)
+            return
+        if key > 0:
+            dx[("l", key - 1)].wait_recv()
+            tot = tot + dxl[key - 1][...].astype(F32)
+        wg_ref[:, c0:c1] = tot.astype(BF16)
+        put_out(wg_ref.at[:, pl.ds(c0, c1 - c0)], wg_hbm.at[:, pl.ds(c0, c1 - c0)])
 
     def sums_start():
         sms[...] = jnp.zeros_like(sms)
@@ -474,6 +489,7 @@
         for k in range(1, NB):
             total = total + smr[k]
         small_ref[...] = total
+        put_out(small_ref, small_hbm)
 
     sm_copies = []
     steps = []
@@ -539,14 +555,14 @@
     do(c_plane1, 1, 7)
     do(d_own1, 2)
     do(d_core, 0, 2)
+    do(c_plane1, 1, 5)
     do(c_plane1, 1, 3)
-    do(c_plane1, 1, 5)
     do(c_add1, 1, 1)
+    do(d_core, 1, 1)
     do(c_start0, 1)
     do(c_plane1, 1, 2)
     do(sums, 1)
     do(c_plane1, 1, 6)
-    do(d_core, 1, 1)
     do(d_own0, 2)
     do(sums, 0)
     do(c_end1, 0)
@@ -556,10 +572,11 @@
     do(d_core, 0, 3)
     do(c_add1, 1, 2)
     do(c_plane1, 1, 1)
-    do(d_mid, 1)
+    do(d_mid, 3)
     do(d_core, 1, 0)
     do(c_add0, 1, 1)
     do(sums_send)
+    do(d_mid, 1)
     do(d_own1, 0)
     do(d_own0, 3)
     do(d_core, 0, 1)
@@ -576,7 +593,9 @@
     do(d_own0, 0)
     do(d_x0, 0)
     do(d_last, 1)
+    do(d_last, 3)
     do(d_mid, 2)
+    do(d_mid, 4)
     do(d_last, 0)
     do(c_add0, 1, 3)
     do(sums_end)
@@ -584,25 +603,42 @@
     do(c_final, 1)
     do(small_send)
     do(d_last, 2)
+    do(d_last, 4)
     do(small_end)
     for f, a in steps:
         f(*a)
     for c in sends:
         c.wait_send()
-
-
-def place(ctx, ig, wg, small, ctx_out, ig_out, wg_out, ngg_out, qkg_out):
-    ctx_out[...] = ctx[...]
-    ig_out[...] = ig[...]
-    wg_out[...] = wg[...]
+    for c in outs:
+        c.wait()
+
+
+def place(ctx, ig, wg, small, ctx_out, ig_out, wg_out, ngg_out, qkg_out, ctx_v, ig_v, wg_v, small_v, ngg_v, qkg_v, sem):
+    ins = [
+        pltpu.make_async_copy(a, b, sem.at[i])
+        for i, (a, b) in enumerate(((small, small_v), (wg, wg_v), (ig, ig_v), (ctx, ctx_v)))
+    ]
+    outs = [
+        pltpu.make_async_copy(a, b, sem.at[4 + i])
+        for i, (a, b) in enumerate(((wg_v, wg_out), (ig_v, ig_out), (ctx_v, ctx_out), (ngg_v, ngg_out), (qkg_v, qkg_out)))
+    ]
+    for c in ins:
+        c.start()
+    ins[0].wait()
     for i in range(3):
-        ngg_out[pl.ds(i * 128, 128)] = small[i, :]
+        ngg_v[pl.ds(i * 128, 128)] = small_v[i, :]
     for i in range(2):
-        qkg_out[i] = small[3 + 2 * i:5 + 2 * i, :]
+        qkg_v[i] = small_v[3 + 2 * i:5 + 2 * i, :]
+    outs[3].start()
+    outs[4].start()
+    for i in range(3):
+        ins[1 + i].wait()
+        outs[i].start()
+    for c in outs:
+        c.wait()
 
 
 def per_device(patches, norm_gain, qkv_weight, qk_gain, context_grad):
-    vmem = pl.BlockSpec(memory_space=pltpu.VMEM)
     hbm = pl.BlockSpec(memory_space=pl.ANY)
     flops = 2 * TOK * D * HC * 3
     ctx, ig, wg, small = pl.pallas_call(
@@ -614,8 +650,12 @@
             jax.ShapeDtypeStruct((8, 128), F32),
         ),
         in_specs=[hbm] * 5,
-        out_specs=(vmem, vmem, vmem, vmem),
+        out_specs=(hbm,) * 4,
         scratch_shapes=[
+            pltpu.VMEM((TOK, 256), BF16),
+            pltpu.VMEM((TOK, FB), BF16),
+            pltpu.VMEM((FB, HC), BF16),
+            pltpu.VMEM((8, 128), F32),
             pltpu.VMEM((FB,), BF16),
             pltpu.VMEM((2, 2, HEAD_DIM), F32),
             pltpu.VMEM((TOK, 256), BF16),
@@ -637,11 +677,10 @@
             pltpu.VMEM((NIMG, IMG, FB), BF16),
             pltpu.VMEM((NIMG, IMG, FB), BF16),
             pltpu.VMEM((8, FB, HC), BF16),
-            pltpu.VMEM((8, FB, HC), BF16),
             pltpu.VMEM((4, FB, XC), BF16),
-            pltpu.VMEM((FB, HC - XC), BF16),
-            pltpu.VMEM((2, 2, FB, XC), BF16),
-            pltpu.VMEM((2, 2, 2, FB, HC - XC), BF16),
+            pltpu.VMEM((FB, MID - XC), BF16),
+            pltpu.VMEM((FB, HC - MID), BF16),
+            *[pltpu.VMEM((2, 2, FB, c1 - c0), BF16) for _, c0, c1 in STREAMS],
             pltpu.VMEM((8, 128), F32),
             pltpu.VMEM((NB, 8, 128), F32),
             pltpu.VMEM((128, TOK), F32),
@@ -649,10 +688,10 @@
             pltpu.VMEM((NB, 8, 128), F32),
             pltpu.SemaphoreType.DMA((NSEM,)),
             pltpu.SemaphoreType.DMA((NSEM,)),
-            pltpu.SemaphoreType.DMA((6,)),
+            pltpu.SemaphoreType.DMA((16,)),
         ],
         compiler_params=pltpu.CompilerParams(
-            collective_id=0, has_side_effects=True, vmem_limit_bytes=62 * 2**20
+            collective_id=0, has_side_effects=True, vmem_limit_bytes=58 * 2**20
         ),
         cost_estimate=pl.CostEstimate(flops=flops, bytes_accessed=2**25, transcendentals=2**18),
     )(patches, norm_gain, qkv_weight, qk_gain, context_grad)
@@ -665,8 +704,17 @@
             jax.ShapeDtypeStruct((FB,), F32),
             jax.ShapeDtypeStruct((2, 2, HEAD_DIM), F32),
         ),
-        in_specs=[vmem] * 4,
-        out_specs=(vmem,) * 5,
+        in_specs=[hbm] * 4,
+        out_specs=(hbm,) * 5,
+        scratch_shapes=[
+            pltpu.VMEM((TOK, 256), BF16),
+            pltpu.VMEM((TOK, FB), BF16),
+            pltpu.VMEM((FB, HC), BF16),
+            pltpu.VMEM((8, 128), F32),
+            pltpu.VMEM((FB,), F32),
+            pltpu.VMEM((2, 2, HEAD_DIM), F32),
+            pltpu.SemaphoreType.DMA((9,)),
+        ],
     )(ctx, ig, wg, small)
 
 

time: 124 us -> 123 us (level)
  no operation moved by 1% of the time
where the time goes in v4:
time: 123 us
  Pallas kernels  122 us (99%)
    pallas_call x1, Pallas kernels, per_device(): pl.pallas_call(kernel, out_shape=(jax.ShapeDtypeStruct((TOK, 256), BF16),...  120 us

profile of v4, /device:TPU:1, one launch (start us, length us, event | category | flops | bytes accessed | tf_op | source)
XLA Modules:
  0.0 123.2 jit_solution(6547364465860359901)
XLA Ops:
  0.6 120.2 %shard_map.92 = (bf16[512,256]{1,0:T(8,128)(2,1)}, bf16[512,384]{1,0:T(8,128)(2,1)}, bf16[384,768]{1,0:T(8,128)(2,1)}, f32[8,128]{1,0:T(8,128)}) custom-call(bf16[512,384]{1,0:T(8,128)(2,1)} %p_hbm.1, bf16[384]{0:T(512)(128)(2,1)} %gain_hbm.1, bf16[6144,768]{1,0:T(8,128)(2,1)} %w_hbm.1, f32[2,2,128]{2,1,0:T(2,128)} %qkg_hbm.1, bf16[512,256]{1,0:T(8,128)(2,1)} %cg_hbm.1), custom_call_target="tpu_custom_call" | custom-call | flops 14495514624 | bytes 33554432 | tf_op jit(solution)/shard_map/pallas_call | solution.py:644
  120.9 2.2 %shard_map.93 = (bf16[512,256]{1,0:T(8,128)(2,1)}, bf16[512,384]{1,0:T(8,128)(2,1)}, bf16[384,768]{1,0:T(8,128)(2,1)}, f32[384]{0:T(512)}, f32[2,2,128]{2,1,0:T(2,128)}) custom-call(bf16[512,256]{1,0:T(8,128)(2,1)} %get-tuple-element.9.ctx, bf16[512,384]{1,0:T(8,128)(2,1)} %get-tuple-element.10.ig, bf16[384,768]{1,0:T(8,128)(2,1)} %get-tuple-element.11.wg, ...), custom_call_target="tpu_custom_call" | custom-call | tf_op jit(solution)/shard_map/pallas_call | solution.py:698
